TPU v7x, 512 devices: a whole 4x4x16 slice. The times are simulated.
512 devices in a mesh: section: 32 (over x_lo, z), tensor: 16 (over y, x_hi, core).
Axes of the slice: x: 4 (x_hi: 2, x_lo: 2; x = x_hi * 2 + x_lo), y: 4, z: 16, core: 2. Of those that a mesh axis runs over, the one named last changes fastest.
Arguments:
- section_input: bfloat16 [32, 128, 3072], P('section', 'tensor'), may hold values from -6 to 6
- query: bfloat16 [32, 3072, 128], P('section', 'tensor'), may hold values from -100 to 100
- key_stash: bfloat16 [32, 3072, 128], P('section', 'tensor'), may hold values from -4 to 4
- incoming: bfloat16 [32, 128, 3072], P('section', 'tensor'), may hold values from -6 to 6
- version: int32 [32], P('section'), may hold values from 0 to 1
- w_value: bfloat16 [32, 2, 3072, 1536], P('section', None, 'tensor'), may hold values from -0.109375 to 0.109375
- w_out: bfloat16 [32, 2, 3072, 1536], P('section', None, 'tensor'), may hold values from -0.109375 to 0.109375
Outputs:
- input_grad: bfloat16 [32, 128, 3072], P('section', 'tensor')
- grad_value: bfloat16 [32, 3072, 1536], P('section', 'tensor')
- grad_out: bfloat16 [32, 3072, 1536], P('section', 'tensor')
All inputs are finite; a program needn't handle non-finite values.
Results may differ from a plain program's by a relative error of at most 0.018.
Values may be sent and summed in bfloat16 or wider, within the bound.
A program may use at most 64 MiB of HBM per device.

v0:
```python
import math

import jax
import jax.numpy as jnp
from jax import lax
from jax.sharding import PartitionSpec as P

HEAD_DIM = 96


def from_partner(array, axis, bit):
    return lax.ppermute(array, axis, [(i, i ^ 1 << bit) for i in range(lax.axis_size(axis))])


def shifted(value, axis, steps):
    count = lax.axis_size(axis)
    leading, last = (max(0, -steps), min(count, count - steps))
    return lax.ppermute(value, axis, [(source, source + steps) for source in range(leading, last)])


def contract_rows(left_side, right_side):
    return lax.dot_general(
        left_side, right_side, (((0,), (0,)), ((), ())), preferred_element_type=jnp.float32
    )


def on_device(section_input, query, key_stash, incoming, version, w_value, w_out):
    position = lax.axis_index("section")
    parity = position % 2
    section_parity = position // 2 % 2
    chosen = version[0]
    stacked = jnp.stack([w_value[0], w_out[0]])
    own_halves = lax.dynamic_index_in_dim(stacked, chosen, 1, keepdims=False)
    partner = from_partner(stacked, "section", 0)
    theirs = lax.dynamic_index_in_dim(partner, chosen, 1, keepdims=False)
    left_part = jnp.where(parity == 0, own_halves, theirs)
    right_part = jnp.where(parity == 0, theirs, own_halves)
    weights = jnp.concatenate([left_part, right_part], axis=2)
    value_weight = weights[0]
    out_weight = weights[1]
    local_rows = value_weight.shape[0]
    width = value_weight.shape[1]
    tokens = query.shape[2]
    local_heads = local_rows // HEAD_DIM
    shard_rows = section_input.shape[1]
    full_input = lax.all_gather(section_input[0], "tensor", axis=0, tiled=True)
    values = lax.dot_general(
        value_weight, full_input, (((1,), (1,)), ((), ())), preferred_element_type=jnp.float32
    ).astype(jnp.bfloat16)
    query_heads = query[0].reshape(local_heads, HEAD_DIM, tokens)
    key_heads = key_stash[0].reshape(local_heads, HEAD_DIM, tokens)
    scores = jnp.einsum(
        "hdi,hdj->hij", query_heads, key_heads, preferred_element_type=jnp.float32
    ) * (1.0 / math.sqrt(HEAD_DIM))
    causal = lax.broadcasted_iota(jnp.int32, (tokens, tokens), 1) <= lax.broadcasted_iota(
        jnp.int32, (tokens, tokens), 0
    )
    scores = jnp.where(causal, scores, -jnp.inf)
    row_max = jnp.max(scores, axis=2, keepdims=True)
    expo = jnp.exp(scores - row_max)
    attend = (expo / jnp.sum(expo, axis=2, keepdims=True)).astype(jnp.bfloat16)
    value_heads = values.reshape(local_heads, HEAD_DIM, tokens)
    context = (
        jnp.einsum("hdj,hij->hdi", value_heads, attend, preferred_element_type=jnp.float32)
        .astype(jnp.bfloat16)
        .reshape(local_rows, tokens)
    )
    value_wgrad = jnp.zeros((local_rows, width), jnp.float32)
    out_wgrad = jnp.zeros((local_rows, width), jnp.float32)
    received = incoming[0]
    first_dx = incoming[0]
    input_grad = incoming[0]
    for section_round in range(2):
        if section_round == 0:
            grad_shard = incoming[0]
            active = section_parity == 1
        else:
            grad_shard = received
            active = section_parity == 0
        full_grad = lax.all_gather(grad_shard, "tensor", axis=0, tiled=True)

        def backward_terms(upstream_full):
            context_grad = lax.dot_general(
                out_weight,
                upstream_full,
                (((1,), (1,)), ((), ())),
                preferred_element_type=jnp.float32,
            ).astype(jnp.bfloat16)
            context_heads = context_grad.reshape(local_heads, HEAD_DIM, tokens)
            value_grad = (
                jnp.einsum(
                    "hdi,hij->hdj", context_heads, attend, preferred_element_type=jnp.float32
                )
                .astype(jnp.bfloat16)
                .reshape(local_rows, tokens)
            )
            value_term = jnp.dot(value_grad, full_input, preferred_element_type=jnp.float32)
            out_term = jnp.dot(context, upstream_full, preferred_element_type=jnp.float32)
            return (value_grad, value_term, out_term)

        def skipped(upstream_full):
            return (
                jnp.zeros((local_rows, tokens), jnp.bfloat16),
                jnp.zeros((local_rows, width), jnp.float32),
                jnp.zeros((local_rows, width), jnp.float32),
            )

        value_grad, value_term, out_term = lax.cond(active, backward_terms, skipped, full_grad)
        value_wgrad = value_wgrad + value_term
        out_wgrad = out_wgrad + out_term
        mine_rows = lax.psum_scatter(
            lax.cond(
                active,
                lambda piece_now: contract_rows(piece_now, value_weight),
                lambda piece_now: jnp.zeros(
                    (shard_rows * lax.axis_size("tensor"), width), jnp.float32
                ),
                value_grad,
            ).astype(jnp.bfloat16),
            "tensor",
            scatter_dimension=0,
            tiled=True,
        ).astype(jnp.float32)
        dx_shard = (grad_shard.astype(jnp.float32) + mine_rows).astype(jnp.bfloat16)
        if section_round == 0:
            first_dx = dx_shard
            received = shifted(dx_shard, "section", -2)
        else:
            input_grad = jnp.where(section_parity == 1, first_dx, dx_shard)
    half_width = width // 2
    both_grads = jnp.stack([value_wgrad, out_wgrad])
    kept_half = jnp.where(parity == 0, both_grads[:, :, :half_width], both_grads[:, :, half_width:])
    sent_half = jnp.where(parity == 0, both_grads[:, :, half_width:], both_grads[:, :, :half_width])
    arrived = from_partner(sent_half.astype(jnp.bfloat16), "section", 0).astype(sent_half.dtype)
    summed_grads = (kept_half + arrived).astype(jnp.bfloat16)
    return (input_grad[None], summed_grads[0][None], summed_grads[1][None])


def solution(mesh):
    placed = (
        P("section", "tensor", None),
        P("section", "tensor", None),
        P("section", "tensor", None),
        P("section", "tensor", None),
        P("section"),
        P("section", None, "tensor", None),
        P("section", None, "tensor", None),
    )
    return jax.shard_map(
        on_device,
        mesh=mesh,
        in_specs=placed,
        out_specs=(
            P("section", "tensor", None),
            P("section", "tensor", None),
            P("section", "tensor", None),
        ),
        check_vma=False,
    )
```

profile of v0, /device:TPU:1, one launch (start us, length us, event | category | flops | bytes accessed | tf_op | source)
XLA Modules:
  0.0 313.0 jit_solution(14765387359347611891)
XLA Ops:
  7.2 0.0 copy-start
  7.2 0.0 reduce-scatter.3.cloned.1.call-start
  7.2 0.0 copy-start.11
  7.2 0.0 copy-start.10
  7.2 0.0 copy-start.9
  7.3 0.0 copy-start.6
  7.3 0.0 copy-start.7
  7.3 3.4 %pad_maximum_fusion = bf16[2,2,192,1536]{3,2,0,1:T(8,128)(2,1)} fusion(bf16[1,2,192,1536]{3,2,0,1:T(8,128)(2,1)} %bitcast.64, bf16[1,2,192,1536]{3,2,0,1:T(8,128)(2,1)} %bitcast.66), kind=kLoop, calls=%fused_computation.8 | loop fusion | flops 1179648 | bytes 4718592 | tf_op jit(solution)/shard_map/stack | solution.py:32
  10.7 4.4 %collective-permute-start = (bf16[2,2,192,1536]{3,2,0,1:T(8,128)(2,1)}, bf16[2,2,192,1536]{3,2,0,1:T(8,128)(2,1)}, u32[]{:S(2)}, u32[]{:S(2)}) collective-permute-start(bf16[2,2,192,1536]{3,2,0,1:T(8,128)(2,1)} %pad_maximum_fusion), channel_id=1, source_target_pairs={{0,16},{16,0},{32,48},{48,32},{64,80},{80,64},{96,112},{112,96},{1... | collective-permute-start | bytes 7077896 | tf_op jit(solution)/shard_map/ppermute | solution.py:12
  15.8 0.0 copy-done
  15.8 0.0 copy-done.11
  15.8 0.3 fusion.17
  16.1 0.0 copy-done.10
  16.1 28.9 %all-gather.1 = bf16[1,128,3072]{2,1,0:T(8,128)(2,1)S(1)} all-gather(bf16[1,8,3072]{2,1,0:T(8,128)(2,1)S(1)} %copy-done.10), channel_id=3, replica_groups=mesh['section'=32,'tensor'=16] {'tensor'}, dimensions={1}, use_global_device_ids=true | all-gather | bytes 835584 | tf_op jit(solution)/shard_map/all_gather | solution.py:46
  45.1 0.0 copy-done.9
  45.1 24.0 %all-gather = bf16[1,128,3072]{2,1,0:T(8,128)(2,1)S(1)} all-gather(bf16[1,8,3072]{2,1,0:T(8,128)(2,1)S(1)} %copy-done.9), channel_id=2, replica_groups=mesh['section'=32,'tensor'=16] {'tensor'}, dimensions={1}, use_global_device_ids=true | all-gather | bytes 835584 | tf_op jit(solution)/shard_map/all_gather | solution.py:80
  69.1 0.0 collective-permute-done
  69.1 0.0 copy-done.6
  69.1 0.0 copy-done.7
  69.1 1.4 select_bitcast_fusion
  70.6 0.3 fusion.5
  70.8 0.0 copy-start.2
  70.9 0.5 convolution_convert_fusion.5
  71.3 0.1 convolution_convert_fusion.4
  71.5 2.6 conditional.4
  71.5 0.6 broadcast.20
  72.1 0.2 broadcast.21.clone
  72.4 1.7 broadcast.21
  74.1 0.0 copy-start.3
  74.1 0.0 copy-done.2
  74.1 1.4 copy-done.3
  75.6 1.0 conditional.5
  75.6 1.0 broadcast.22
  76.5 0.0 reduce-scatter.3.cloned.1.call-update
  76.6 0.0 reduce-scatter.5.cloned.1.call-start
  76.6 91.5 %reduce-scatter.3.cloned.1.call-done = bf16[8,3072]{1,0:T(8,128)(2,1)} async-done(((bf16[128,3072]{1,0:T(8,128)(2,1)}), bf16[8,3072]{1,0:T(8,128)(2,1)}) %reduce-scatter.3.cloned.1.call-update) | async-done | bytes 49168 | tf_op jit(solution)/shard_map/reduce_scatter | solution.py:111
  168.2 0.8 fusion.9
  169.0 1.3 collective-permute-start.1
  170.3 4.4 %collective-permute-done.1 = bf16[8,3072]{1,0:T(8,128)(2,1)S(1)} collective-permute-done((bf16[8,3072]{1,0:T(8,128)(2,1)S(1)}, bf16[8,3072]{1,0:T(8,128)(2,1)S(1)}, u32[]{:S(2)}, u32[]{:S(2)}) %collective-permute-start.1) | collective-permute-done | bytes 49184 | tf_op jit(solution)/shard_map/ppermute | solution.py:18
  174.7 28.7 %all_gather.11 = bf16[128,3072]{1,0:T(8,128)(2,1)S(1)} all-gather(bf16[8,3072]{1,0:T(8,128)(2,1)S(1)} %collective-permute-done.1), channel_id=1, replica_groups=mesh['section'=32,'tensor'=16] {'tensor'}, dimensions={0}, use_global_device_ids=true | all-gather | bytes 835584 | tf_op jit(solution)/shard_map/all_gather | solution.py:80
  203.4 3.0 conditional.6
  203.4 0.5 convolution_convert_fusion.3
  203.9 0.8 convolution_convert_fusion.2
  204.6 0.5 fusion.23
  205.1 1.3 fusion.22
  206.4 0.0 copy-start.4
  206.4 0.0 copy-start.5
  206.4 1.4 copy-done.4
  207.8 0.7 copy-done.5
  208.5 4.5 %add_bitcast_fusion = (f32[1,192,3072]{2,1,0:T(8,128)S(1)}, f32[1,192,3072]{2,1,0:T(8,128)S(1)}) fusion(f32[192,3072]{1,0:T(8,128)} %copy-done.3, f32[192,3072]{1,0:T(8,128)} %copy-done.4, f32[192,3072]{1,0:T(8,128)} %get-tuple-element.59, f32[192,3072]{1,0:T(8,128)} %copy-done.5), kind=kLoop, calls=%fused_computation.16 | loop fusion | flops 1179648 | bytes 14155776 | tf_op jit(solution)/shard_map/stack | solution.py:131
  213.0 0.0 copy-start.1
  213.0 1.7 select_convert_fusion
  214.8 0.1 copy-done.1
  214.9 3.2 %collective-permute-start.2 = (bf16[2,192,1536]{2,1,0:T(8,128)(2,1)}, bf16[2,192,1536]{2,1,0:T(8,128)(2,1)}, u32[]{:S(2)}, u32[]{:S(2)}) collective-permute-start(bf16[2,192,1536]{2,1,0:T(8,128)(2,1)} %select_convert_fusion), channel_id=1, source_target_pairs={{0,16},{16,0},{32,48},{48,32},{64,80},{80,64},{96,112},{112,96},{1... | collective-permute-start | bytes 3538952 | tf_op jit(solution)/shard_map/ppermute | solution.py:12
  218.1 1.7 conditional.7
  218.1 1.7 fusion.19
  219.8 0.0 copy-start.8
  219.8 0.9 copy-done.8
  220.7 0.0 reduce-scatter.5.cloned.1.call-update
  220.8 23.8 %collective-permute-done.2 = bf16[2,192,1536]{2,1,0:T(8,128)(2,1)} collective-permute-done((bf16[2,192,1536]{2,1,0:T(8,128)(2,1)}, bf16[2,192,1536]{2,1,0:T(8,128)(2,1)}, u32[]{:S(2)}, u32[]{:S(2)}) %collective-permute-start.2) | collective-permute-done | bytes 1179680 | tf_op jit(solution)/shard_map/ppermute | solution.py:12
  244.5 2.6 add_convert_fusion
  247.2 1.1 fusion.16
  248.3 56.5 %reduce-scatter.5.cloned.1.call-done = bf16[8,3072]{1,0:T(8,128)(2,1)} async-done(((bf16[128,3072]{1,0:T(8,128)(2,1)}), bf16[8,3072]{1,0:T(8,128)(2,1)}) %reduce-scatter.5.cloned.1.call-update) | async-done | bytes 49168 | tf_op jit(solution)/shard_map/reduce_scatter | solution.py:111
  304.7 1.4 fusion.11
  (2 shorter events, 0.0 us)
Async XLA Ops:
  7.2 8.6 %copy-start = (bf16[1,192,128]{2,1,0:T(8,128)(2,1)S(1)}, bf16[1,192,128]{2,1,0:T(8,128)(2,1)}, u32[]{:S(2)}) copy-start(bf16[1,192,128]{2,1,0:T(8,128)(2,1)} %param.16) | copy-start | bytes 147460
  7.2 161.0 %reduce-scatter.3.cloned.1.call-start = ((), (), s32[]{:S(2)}) async-start(), calls=%async_computation.2 | async-start | bytes 835584 | tf_op jit(solution)/shard_map/reduce_scatter | solution.py:111
  7.2 8.6 %copy-start.11 = (bf16[1,192,128]{2,1,0:T(8,128)(2,1)S(1)}, bf16[1,192,128]{2,1,0:T(8,128)(2,1)}, u32[]{:S(2)}) copy-start(bf16[1,192,128]{2,1,0:T(8,128)(2,1)} %param.17) | copy-start | bytes 147460
  7.2 8.9 %copy-start.10 = (bf16[1,8,3072]{2,1,0:T(8,128)(2,1)S(1)}, bf16[1,8,3072]{2,1,0:T(8,128)(2,1)}, u32[]{:S(2)}) copy-start(bf16[1,8,3072]{2,1,0:T(8,128)(2,1)} %param.15) | copy-start | bytes 147460
  7.2 37.8 %copy-start.9 = (bf16[1,8,3072]{2,1,0:T(8,128)(2,1)S(1)}, bf16[1,8,3072]{2,1,0:T(8,128)(2,1)}, u32[]{:S(2)}) copy-start(bf16[1,8,3072]{2,1,0:T(8,128)(2,1)} %param.18) | copy-start | bytes 147460
  7.3 61.9 %copy-start.6 = (bf16[1,2,192,1536]{3,2,1,0:T(8,128)(2,1)S(1)}, bf16[1,2,192,1536]{3,2,1,0:T(8,128)(2,1)}, u32[]{:S(2)}) copy-start(bf16[1,2,192,1536]{3,2,1,0:T(8,128)(2,1)} %param.21) | copy-start | bytes 3538948
  7.3 61.9 %copy-start.7 = (bf16[1,2,192,1536]{3,2,1,0:T(8,128)(2,1)S(1)}, bf16[1,2,192,1536]{3,2,1,0:T(8,128)(2,1)}, u32[]{:S(2)}) copy-start(bf16[1,2,192,1536]{3,2,1,0:T(8,128)(2,1)} %param.20) | copy-start | bytes 3538948
  10.7 58.4 %collective-permute-start = (bf16[2,2,192,1536]{3,2,0,1:T(8,128)(2,1)}, bf16[2,2,192,1536]{3,2,0,1:T(8,128)(2,1)}, u32[]{:S(2)}, u32[]{:S(2)}) collective-permute-start(bf16[2,2,192,1536]{3,2,0,1:T(8,128)(2,1)} %pad_maximum_fusion), channel_id=1, source_target_pairs={{0,16},{16,0},{32,48},{48,32},{64,80},{80,64},{96,112},{112,96},{1... | collective-permute-start | bytes 7077896 | tf_op jit(solution)/shard_map/ppermute | solution.py:12
  70.8 3.3 %copy-start.2 = (bf16[192,3072]{1,0:T(8,128)(2,1)}, bf16[192,3072]{1,0:T(8,128)(2,1)S(1)}, u32[]{:S(2)}) copy-start(bf16[192,3072]{1,0:T(8,128)(2,1)S(1)} %get-tuple-element.75) | copy-start | bytes 3538948
  74.1 1.4 copy-start.3
  76.6 228.2 %reduce-scatter.5.cloned.1.call-start = ((), (), s32[]{:S(2)}) async-start(), calls=%async_computation.3 | async-start | bytes 835584 | tf_op jit(solution)/shard_map/reduce_scatter | solution.py:111
  169.0 5.7 %collective-permute-start.1 = (bf16[8,3072]{1,0:T(8,128)(2,1)S(1)}, bf16[8,3072]{1,0:T(8,128)(2,1)S(1)}, u32[]{:S(2)}, u32[]{:S(2)}) collective-permute-start(bf16[8,3072]{1,0:T(8,128)(2,1)S(1)} %fusion.9), channel_id=1, source_target_pairs={{32,0},{48,16},{64,32},{80,48},{96,64},{112,80},{128,96},{144,112}... | collective-permute-start | bytes 147464 | tf_op jit(solution)/shard_map/ppermute | solution.py:18
  206.4 1.4 copy-start.4
  206.4 2.2 copy-start.5
  213.0 1.9 copy-start.1
  214.9 29.6 %collective-permute-start.2 = (bf16[2,192,1536]{2,1,0:T(8,128)(2,1)}, bf16[2,192,1536]{2,1,0:T(8,128)(2,1)}, u32[]{:S(2)}, u32[]{:S(2)}) collective-permute-start(bf16[2,192,1536]{2,1,0:T(8,128)(2,1)} %select_convert_fusion), channel_id=1, source_target_pairs={{0,16},{16,0},{32,48},{48,32},{64,80},{80,64},{96,112},{112,96},{1... | collective-permute-start | bytes 3538952 | tf_op jit(solution)/shard_map/ppermute | solution.py:12
  219.8 0.9 copy-start.8
Sparse Core Ops, SparseCore 0:
  76.7 91.4 reduce-scatter.2
  220.9 83.8 reduce-scatter.4
where the time goes:
time: 314 us; the launch traced here: 313 us
  waiting for transfers between devices  176 us (56%)
  blocking collectives  81.7 us (26%)
  other arithmetic  16.3 us (5%)
  between operations  14.9 us (5%)
  local copies, waits for them, and re-layouts  9.33 us (3%)
  starting transfers between devices  8.92 us (3%)
  matrix products  5.53 us (2%)
    reduce_scatter x2, waiting for transfers between devices, on_device(): lax.psum_scatter(lax.cond(active, lambda piece_now: contract_rows(piece_n...  148 us
    all_gather x2, blocking collectives, on_device(): full_grad = lax.all_gather(grad_shard, 'tensor', axis=0, tiled=True)  52.7 us
    all_gather x1, blocking collectives, on_device(): full_input = lax.all_gather(section_input[0], 'tensor', axis=0, tiled=True)  28.9 us
    ppermute x2, waiting for transfers between devices, from_partner(): lax.ppermute(array, axis, [(i, i ^ 1 << bit) for i in range(lax.axis_size...  23.8 us
    ppermute x2, starting transfers between devices, from_partner(): lax.ppermute(array, axis, [(i, i ^ 1 << bit) for i in range(lax.axis_size...  7.55 us
  transfers between devices with their start and end apart: 5, of which 4 were waited for; matrix products, arithmetic and copies ran while one was open for 2% of the time, Pallas kernels for 0%

commit v1 on v0

v1 whole, which is shorter than its diff:
```python
import functools
import math

import jax
import jax.numpy as jnp
from jax import lax
from jax.experimental import pallas as pl
from jax.experimental.pallas import tpu as pltpu
from jax.sharding import PartitionSpec as P

HEAD_DIM = 96
BF16 = jnp.bfloat16
F32 = jnp.float32
MESH = pl.DeviceIdType.MESH


def dot(left, right, left_dim, right_dim):
    return lax.dot_general(
        left, right, (((left_dim,), (right_dim,)), ((), ())), preferred_element_type=F32
    )


def kernel(
    count,
    x_ref, query_ref, key_ref, incoming_ref, version_ref, wv_ref, wo_ref,
    dx_ref, gv_ref, go_ref,
    wv, wo, query, key, probs, versions,
    grad_own, grad_in, x_in, grad_full, x_full,
    values_own, values_sent, values_got, grads_own, grads_sent, grads_got,
    context, value_grad, dx_parts, dx_got, dx_own, gv, go,
    load_sem, pair_send, pair_recv, x_send, x_recv, grad_send, grad_recv,
    dx_send, dx_recv, shift_send, shift_recv, out_sem,
):
    section = lax.axis_index("section")
    tensor = lax.axis_index("tensor")
    mine = lax.rem(section, 2)
    base = section - mine
    partner = base + 1 - mine
    odd = lax.rem(section // 2, 2)
    other = section + 2 - 4 * odd
    rows = wv.shape[1]
    half = wv.shape[2]
    heads = rows // HEAD_DIM
    shard = grad_own.shape[0]
    tokens = count * shard
    tile = half // 3 if half % 384 == 0 else half
    own_slot = mine * count + tensor

    def peer(step):
        return lax.rem(tensor + step, count)

    def columns(which):
        return pl.ds(pl.multiple_of(which * half, half), half)

    loads = [
        pltpu.make_async_copy(query_ref.at[0], query, load_sem.at[0]),
        pltpu.make_async_copy(key_ref.at[0], key, load_sem.at[1]),
        pltpu.make_async_copy(wo_ref.at[0], wo, load_sem.at[2]),
        pltpu.make_async_copy(wv_ref.at[0], wv, load_sem.at[3]),
    ]
    own_load = pltpu.make_async_copy(incoming_ref.at[0], grad_own, load_sem.at[4])
    for load in loads:
        load.start()
    pl.when(odd == 1)(own_load.start)

    barrier = pltpu.get_barrier_semaphore()

    def greet(target, first):
        def step(j, carry):
            pl.semaphore_signal(
                barrier, inc=1, device_id=(target, peer(j)), device_id_type=MESH
            )
            return carry

        lax.fori_loop(first, count, step, 0)

    pl.semaphore_signal(barrier, inc=1, device_id=(other, tensor), device_id_type=MESH)
    greet(section, 1)
    greet(partner, 0)
    pl.semaphore_wait(barrier, 2 * count)

    def send_to(target, first, source, destination, send, recv):
        def step(j, carry):
            pltpu.make_async_remote_copy(
                src_ref=source(peer(j)),
                dst_ref=destination,
                send_sem=send,
                recv_sem=recv,
                device_id=(target, peer(j)),
                device_id_type=MESH,
            ).start()
            return carry

        lax.fori_loop(first, count, step, 0)

    def gather_start(source, buffer, send, recv):
        slot = buffer.at[own_slot]
        send_to(section, 1, lambda _: source.at[:, columns(mine)], slot, send, recv)
        send_to(partner, 0, lambda _: source.at[:, columns(1 - mine)], slot, send, recv)
        pltpu.make_async_copy(source.at[:, columns(mine)], slot, recv).start()

    def wait_all(buffer, sem):
        pltpu.make_async_copy(buffer, buffer, sem).wait()

    def wait_sent(buffer, sem):
        sent = buffer.at[pl.ds(0, 2 * count - 1)]
        pltpu.make_async_copy(sent, sent, sem).wait()

    def flatten(buffer, full):
        def step(i, carry):
            block = buffer[pl.ds(2 * i, 2)].astype(F32).reshape(2 * shard, half)
            full[pl.ds(pl.multiple_of(i * 2 * shard, 2 * shard), 2 * shard), :] = block.astype(BF16)
            return carry

        lax.fori_loop(0, count, step, 0)

    def to_partner(source, destination, index):
        return pltpu.make_async_remote_copy(
            src_ref=source,
            dst_ref=destination,
            send_sem=pair_send.at[index],
            recv_sem=pair_recv.at[index],
            device_id=(partner, tensor),
            device_id_type=MESH,
        )

    send_probs = to_partner(probs.at[mine], probs.at[mine], 0)
    send_version = to_partner(versions.at[mine], versions.at[mine], 1)
    send_values = to_partner(values_sent, values_got, 2)
    send_grads = to_partner(grads_sent, grads_got, 3)
    shift = pltpu.make_async_remote_copy(
        src_ref=dx_own,
        dst_ref=grad_own,
        send_sem=shift_send,
        recv_sem=shift_recv,
        device_id=(other, tensor),
        device_id_type=MESH,
    )

    def attention():
        versions[mine] = jnp.full(versions.shape[1:], version_ref[0], jnp.int32)
        send_version.start()
        loads[0].wait()
        loads[1].wait()
        row = lax.broadcasted_iota(jnp.int32, (tokens, tokens), 0)
        causal = lax.broadcasted_iota(jnp.int32, (tokens, tokens), 1) <= row
        for head in range(heads):
            part = slice(head * HEAD_DIM, (head + 1) * HEAD_DIM)
            scores = dot(query[part], key[part], 0, 0) * (1.0 / math.sqrt(HEAD_DIM))
            scores = jnp.where(causal, scores, -jnp.inf)
            expo = jnp.exp(scores - jnp.max(scores, axis=1, keepdims=True))
            attend = expo / jnp.sum(expo, axis=1, keepdims=True)
            probs[mine, head] = attend.astype(BF16)
        send_probs.start()
        send_version.wait()
        send_probs.wait()
        loads[2].wait()
        loads[3].wait()

    def chosen(which):
        return jnp.max(versions[which])

    def token_rows(which):
        return slice(which * tokens, (which + 1) * tokens)

    def project(weight, full, own, sent):
        for which in range(2):
            partial = dot(weight[chosen(which)], full[token_rows(which)], 1, 1)
            own[which] = partial
            sent[which] = partial.astype(BF16)

    def mix(own, got, out, side):
        for which in range(2):
            for head in range(heads):
                part = slice(head * HEAD_DIM, (head + 1) * HEAD_DIM)
                whole = (own[which, part] + got[which, part].astype(F32)).astype(BF16)
                mixed = dot(whole, probs[which, head], 1, side)
                out[part, token_rows(which)] = mixed.astype(BF16)

    def forward_half():
        gather_start(x_ref.at[0], x_in, x_send, x_recv)

    def context_phase():
        wait_all(x_in, x_recv)
        flatten(x_in, x_full)
        project(wv, x_full, values_own, values_sent)
        send_values.start()
        send_values.wait()
        mix(values_own, values_got, context, 1)

    def gradient_phase():
        wait_all(grad_in, grad_recv)
        flatten(grad_in, grad_full)
        project(wo, grad_full, grads_own, grads_sent)
        send_grads.start()
        send_grads.wait()
        mix(grads_own, grads_got, value_grad, 0)
        for which in range(2):
            weight = wv.at[chosen(which)]
            for start in range(0, half, tile):
                part = dot(value_grad[:, token_rows(which)], weight[:, start:start + tile], 0, 0)
                dx_parts[which * count:(which + 1) * count, :, start:start + tile] = part.reshape(
                    count, shard, tile
                ).astype(BF16)
            send_to(
                base + which,
                jnp.where(mine == which, 1, 0),
                lambda to: dx_parts.at[which * count + to],
                dx_got.at[own_slot],
                dx_send,
                dx_recv,
            )
        pltpu.make_async_copy(dx_parts.at[own_slot], dx_got.at[own_slot], dx_recv).start()

    def reduce_phase():
        wait_all(dx_got, dx_recv)
        for side in range(2):
            part = slice(side * half, (side + 1) * half)
            total = dx_got[side * count].astype(F32)
            for slot in range(1, count):
                total = total + dx_got[side * count + slot].astype(F32)
            dx_own[:, part] = (grad_own[:, part].astype(F32) + total).astype(BF16)
        pltpu.make_async_copy(dx_own, dx_ref.at[0], out_sem.at[0]).start()

    def weight_phase():
        for start in range(0, half, tile):
            part = slice(start, start + tile)
            gv[:, part] = dot(value_grad[...], x_full[:, part], 1, 0).astype(BF16)
        pltpu.make_async_copy(gv, gv_ref.at[0], out_sem.at[1]).start()
        for start in range(0, half, tile):
            part = slice(start, start + tile)
            go[:, part] = dot(context[...], grad_full[:, part], 1, 0).astype(BF16)
        pltpu.make_async_copy(go, go_ref.at[0], out_sem.at[2]).start()

    def odd_section():
        gather_start(incoming_ref.at[0], grad_in, grad_send, grad_recv)
        attention()
        gradient_phase()
        own_load.wait()
        reduce_phase()
        shift.start()
        forward_half()
        context_phase()
        weight_phase()
        shift.wait_send()

    def even_section():
        forward_half()
        attention()
        context_phase()
        shift.wait_recv()
        gather_start(grad_own, grad_in, grad_send, grad_recv)
        gradient_phase()
        weight_phase()
        reduce_phase()

    pl.when(odd == 1)(odd_section)
    pl.when(odd == 0)(even_section)
    wait_sent(x_in, x_send)
    wait_sent(grad_in, grad_send)
    wait_sent(dx_parts, dx_send)
    pltpu.make_async_copy(dx_own, dx_ref.at[0], out_sem.at[0]).wait()
    pltpu.make_async_copy(gv, gv_ref.at[0], out_sem.at[1]).wait()
    pltpu.make_async_copy(go, go_ref.at[0], out_sem.at[2]).wait()


def on_device(section_input, query, key_stash, incoming, version, w_value, w_out):
    count = lax.axis_size("tensor")
    shard, width = section_input.shape[1:]
    rows, tokens = query.shape[1:]
    half = width // 2
    heads = rows // HEAD_DIM
    anywhere = pl.BlockSpec(memory_space=pl.ANY)
    pair = (2, rows, tokens)
    blocks = (2 * count, shard, half)
    dma = pltpu.SemaphoreType.DMA
    return pl.pallas_call(
        functools.partial(kernel, count),
        out_shape=(
            jax.ShapeDtypeStruct((1, shard, width), BF16),
            jax.ShapeDtypeStruct((1, rows, half), BF16),
            jax.ShapeDtypeStruct((1, rows, half), BF16),
        ),
        in_specs=[anywhere] * 4 + [pl.BlockSpec(memory_space=pltpu.SMEM)] + [anywhere] * 2,
        out_specs=(anywhere, anywhere, anywhere),
        scratch_shapes=[
            pltpu.VMEM((2, rows, half), BF16),
            pltpu.VMEM((2, rows, half), BF16),
            pltpu.VMEM((rows, tokens), BF16),
            pltpu.VMEM((rows, tokens), BF16),
            pltpu.VMEM((2, heads, tokens, tokens), BF16),
            pltpu.VMEM((2, 8, 128), jnp.int32),
            pltpu.VMEM((shard, width), BF16),
            pltpu.VMEM(blocks, BF16),
            pltpu.VMEM(blocks, BF16),
            pltpu.VMEM((2 * tokens, half), BF16),
            pltpu.VMEM((2 * tokens, half), BF16),
            pltpu.VMEM(pair, F32),
            pltpu.VMEM(pair, BF16),
            pltpu.VMEM(pair, BF16),
            pltpu.VMEM(pair, F32),
            pltpu.VMEM(pair, BF16),
            pltpu.VMEM(pair, BF16),
            pltpu.VMEM((rows, 2 * tokens), BF16),
            pltpu.VMEM((rows, 2 * tokens), BF16),
            pltpu.VMEM(blocks, BF16),
            pltpu.VMEM(blocks, BF16),
            pltpu.VMEM((shard, width), BF16),
            pltpu.VMEM((rows, half), BF16),
            pltpu.VMEM((rows, half), BF16),
            dma((5,)),
            dma((4,)),
            dma((4,)),
            dma,
            dma,
            dma,
            dma,
            dma,
            dma,
            dma,
            dma,
            dma((3,)),
        ],
        compiler_params=pltpu.CompilerParams(
            collective_id=0, has_side_effects=True, vmem_limit_bytes=40 * 1024 * 1024
        ),
    )(section_input, query, key_stash, incoming, version, w_value, w_out)


def solution(mesh):
    split = P("section", "tensor", None)
    weights = P("section", None, "tensor", None)
    return jax.shard_map(
        on_device,
        mesh=mesh,
        in_specs=(split, split, split, split, P("section"), weights, weights),
        out_specs=(split, split, split),
        check_vma=False,
    )
```

time: 314 us -> 82.2 us (0.26)
  waiting for transfers between devices: 176 us -> 0 us
  blocking collectives: 81.7 us -> 0 us
  Pallas kernels: 0 us -> 72.5 us
  other arithmetic: 16.3 us -> 0 us
  between operations: 14.9 us -> 1.3 us
  starting transfers between devices: 8.92 us -> 0 us
  matrix products: 5.53 us -> 0 us
    reduce_scatter x2 -> x0, waiting for transfers between devices: 148 us -> none  [on_device(): lax.psum_scatter(lax.cond(active, lambda piece_now: contract_rows(piece_n...]
    all_gather x3 -> x0, blocking collectives: 81.7 us -> none  [the longest x2 52.7 us: on_device(): full_grad = lax.all_gather(grad_shard, 'tensor', axis=0, tiled=True)]
    pallas_call x0 -> x1, Pallas kernels: none -> 72.5 us  [on_device(): pl.pallas_call(functools.partial(kernel, count), out_shape=(jax.ShapeDtyp...]
    ppermute x3 -> x0, waiting for transfers between devices: 28.2 us -> none  [the longest x2 23.8 us: from_partner(): lax.ppermute(array, axis, [(i, i ^ 1 << bit) for i in range(lax.axis_size...]
    ppermute x3 -> x0, starting transfers between devices: 8.84 us -> none  [the longest x2 7.55 us: from_partner(): lax.ppermute(array, axis, [(i, i ^ 1 << bit) for i in range(lax.axis_size...]
    another operation x2 -> x0, other arithmetic: 7.94 us -> none  [the longest x1 4.5 us: on_device(): both_grads = jnp.stack([value_wgrad, out_wgrad])]
    dot_general x7 -> x0, matrix products: 5.25 us -> none  [the longest x1 1.69 us: contract_rows(): lax.dot_general(left_side, right_side, (((0,), (0,)), ((), ())), preferre...]
    convert_element_type x4 -> x0, other arithmetic: 5.21 us -> none  [the longest x1 2.63 us: on_device(): summed_grads = (kept_half + arrived).astype(jnp.bfloat16)]
  transfers between devices with their start and end apart: 5 -> 0, of which waited for: 4 -> 0; matrix products, arithmetic and copies ran while one was open for 2% -> 0% of each run, Pallas kernels for 0% -> 0%
where the time goes in v1:
time: 82.2 us; the launch traced here: 81.7 us
  Pallas kernels  72.5 us (88%)
  local copies, waits for them, and re-layouts  7.98 us (10%)
  between operations  1.3 us (2%)
    pallas_call x1, Pallas kernels, on_device(): pl.pallas_call(functools.partial(kernel, count), out_shape=(jax.ShapeDtyp...  72.5 us
    unnamed x15, local copies, waits for them, and re-layouts  7.98 us

profile of v1, /device:TPU:1, one launch (start us, length us, event | category | flops | bytes accessed | tf_op | source)
XLA Modules:
  0.0 81.7 jit_solution(18252710482569698836)
XLA Ops:
  1.3 0.0 copy-start
  1.3 1.3 %copy-done = bf16[1,2,192,1536]{3,2,1,0:T(8,128)(2,1)S(1)} copy-done((bf16[1,2,192,1536]{3,2,1,0:T(8,128)(2,1)S(1)}, bf16[1,2,192,1536]{3,2,1,0:T(8,128)(2,1)}, u32[]{:S(2)}) %copy-start) | copy-done | bytes 1179672
  2.5 0.0 copy-start.1
  2.6 1.3 %copy-done.1 = bf16[1,2,192,1536]{3,2,1,0:T(8,128)(2,1)S(1)} copy-done((bf16[1,2,192,1536]{3,2,1,0:T(8,128)(2,1)S(1)}, bf16[1,2,192,1536]{3,2,1,0:T(8,128)(2,1)}, u32[]{:S(2)}) %copy-start.1) | copy-done | bytes 1179672
  3.8 0.0 copy-start.2
  3.8 0.8 copy-done.2
  4.6 0.0 copy-start.3
  4.6 0.8 copy-done.3
  5.4 0.0 copy-start.4
  5.4 0.8 copy-done.4
  6.2 0.0 copy-start.5
  6.2 0.8 copy-done.5
  7.0 72.5 %shard_map.94 = (bf16[1,8,3072]{2,1,0:T(8,128)(2,1)S(1)}, bf16[1,192,1536]{2,1,0:T(8,128)(2,1)S(1)}, bf16[1,192,1536]{2,1,0:T(8,128)(2,1)S(1)}) custom-call(bf16[1,8,3072]{2,1,0:T(8,128)(2,1)S(1)} %copy-done.2, bf16[1,192,128]{2,1,0:T(8,128)(2,1)S(1)} %copy-done.3, bf16[1,192,128]{2,1,0:T(8,128)(2,1)S(1)} %copy-done.4, bf16[1,8,3072]{2,1,0:T(8,128)(2,1)S(1)} %copy-done.5, ...), custom_call_target="tpu_custom_call" | custom-call | tf_op jit(solution)/shard_map/pallas_call | solution.py:277
  79.5 0.6 copy.14
  80.1 0.8 copy.15
  80.9 0.8 copy.16
Async XLA Ops:
  1.3 1.3 %copy-start = (bf16[1,2,192,1536]{3,2,1,0:T(8,128)(2,1)S(1)}, bf16[1,2,192,1536]{3,2,1,0:T(8,128)(2,1)}, u32[]{:S(2)}) copy-start(bf16[1,2,192,1536]{3,2,1,0:T(8,128)(2,1)} %wv_ref.1) | copy-start | bytes 3538948
  2.5 1.3 %copy-start.1 = (bf16[1,2,192,1536]{3,2,1,0:T(8,128)(2,1)S(1)}, bf16[1,2,192,1536]{3,2,1,0:T(8,128)(2,1)}, u32[]{:S(2)}) copy-start(bf16[1,2,192,1536]{3,2,1,0:T(8,128)(2,1)} %wo_ref.1) | copy-start | bytes 3538948
  3.8 0.8 copy-start.2
  4.6 0.8 copy-start.3
  5.4 0.8 copy-start.4
  6.2 0.8 copy-start.5

commit v2 on v1

v2 whole, which is shorter than its diff:
```python
import functools
import math

import jax
import jax.numpy as jnp
from jax import lax
from jax.experimental import pallas as pl
from jax.experimental.pallas import tpu as pltpu
from jax.sharding import PartitionSpec as P

HEAD_DIM = 96
BF16 = jnp.bfloat16
F32 = jnp.float32
MESH = pl.DeviceIdType.MESH


def dot(left, right, left_dim, right_dim):
    return lax.dot_general(
        left, right, (((left_dim,), (right_dim,)), ((), ())), preferred_element_type=F32
    )


def kernel(
    count,
    x_ref, query_ref, key_ref, incoming_ref, version_ref, wv_ref, wo_ref,
    dx_ref, gv_ref, go_ref,
    wv, wo, query, key, probs, versions,
    x_in, grad_in, x_full, grad_full,
    part_x, cast_x, sib_x, total_x, sent_x, got_x, context,
    part_g, cast_g, sib_g, total_g, sent_g, got_g, value_grad,
    parts_odd, got_odd, parts_even, got_even,
    reduced, shifted, pieces, assembled, dx_own, grad_own, gv, go, gv_sent, go_sent,
    load_sem, pair_send, pair_recv, sib_send, sib_recv,
    x_send, x_recv, grad_send, grad_recv, dx_send, dx_recv,
    shift_send, shift_recv, piece_send, piece_recv, own_send, own_recv, out_sem,
):
    section = lax.axis_index("section")
    tensor = lax.axis_index("tensor")
    mine = lax.rem(section, 2)
    base = section - mine
    partner = base + 1 - mine
    odd = lax.rem(section // 2, 2)
    other = section + 2 - 4 * odd
    core = lax.rem(tensor, 2)
    chip = tensor // 2
    sibling = tensor + 1 - 2 * core
    rows = wv.shape[1] // 2
    quarter = wv.shape[2]
    half = 2 * quarter
    heads = rows // HEAD_DIM
    shard = grad_own.shape[0]
    tokens = count * shard
    chips = count // 2
    block = 2 * shard
    own_rows = pl.ds(pl.multiple_of(core * rows, 16), rows)
    sib_rows = pl.ds(pl.multiple_of((1 - core) * rows, 16), rows)

    offsets = [(dy, dx) for dx in (1, 0) for dy in sorted(range(chips // 2), key=lambda d: (-min(d, chips // 2 - d), d))]

    def chip_at(dy, dx):
        side = lax.rem(chip, 2)
        return 2 * lax.rem(chip // 2 + dy, chips // 2) + (1 - side if dx else side)

    def columns(side, which):
        return pl.ds(pl.multiple_of(side * half + which * quarter, 128), quarter)

    def remote(source, destination, send, recv, target, lane):
        return pltpu.make_async_remote_copy(
            src_ref=source,
            dst_ref=destination,
            send_sem=send,
            recv_sem=recv,
            device_id=(target, lane),
            device_id_type=MESH,
        )

    def to_partner(source, destination, index):
        return remote(
            source, destination, pair_send.at[index], pair_recv.at[index], partner, tensor
        )

    def to_sibling(source, destination, index):
        return remote(
            source, destination, sib_send.at[index], sib_recv.at[index], section, sibling
        )

    def wait_all(buffer, sem):
        pltpu.make_async_copy(buffer, buffer, sem).wait()

    loads = [
        pltpu.make_async_copy(query_ref.at[0], query, load_sem.at[0]),
        pltpu.make_async_copy(key_ref.at[0], key, load_sem.at[1]),
        pltpu.make_async_copy(
            wo_ref.at[0, :, :, columns(0, core)], wo.at[:, own_rows], load_sem.at[2]
        ),
        pltpu.make_async_copy(
            wv_ref.at[0, :, :, columns(0, core)], wv.at[:, own_rows], load_sem.at[3]
        ),
    ]
    for load in loads:
        load.start()
    versions[mine] = jnp.full(versions.shape[1:], version_ref[0], jnp.int32)

    barrier = pltpu.get_barrier_semaphore()

    def signal(target, lane):
        pl.semaphore_signal(barrier, inc=1, device_id=(target, lane), device_id_type=MESH)

    def greet(target, first):
        def step(j, carry):
            signal(target, lax.rem(tensor + j, count))
            return carry

        lax.fori_loop(first, count, step, 0)

    signal(other, tensor)
    greet(partner, 0)
    greet(section, 1)
    pl.semaphore_wait(barrier, 2 * count)

    send_version = to_partner(versions.at[mine], versions.at[mine], 0)
    send_probs = to_partner(probs.at[mine], probs.at[mine], 1)
    send_wo = to_sibling(wo_ref.at[0, :, :, columns(0, 1 - core)], wo.at[:, own_rows], 0)
    send_wv = to_sibling(wv_ref.at[0, :, :, columns(0, 1 - core)], wv.at[:, own_rows], 1)

    def gather_start(source, buffer, send, recv):
        slot = buffer.at[mine * count + tensor]
        for dy, dx in offsets:
            for swap in (1, 0):
                lane_core = 1 - core if swap else core
                lane = 2 * chip_at(dy, dx) + lane_core
                remote(
                    source.at[:, columns(1 - mine, lane_core)], slot, send, recv.at[mine], partner, lane
                ).start()
        for dy, dx in offsets:
            for swap in (1, 0):
                if dy or dx or swap:
                    lane_core = 1 - core if swap else core
                    lane = 2 * chip_at(dy, dx) + lane_core
                    remote(
                        source.at[:, columns(mine, lane_core)], slot, send, recv.at[mine], section, lane
                    ).start()
        pltpu.make_async_copy(source.at[:, columns(mine, core)], slot, recv.at[mine]).start()

    def gather_wait(buffer, full, recv, which):
        wait_all(buffer.at[pl.ds(which * count, count)], recv.at[which])

        def step(i, carry):
            pair = buffer[pl.ds(which * count + 2 * i, 2)].astype(F32).reshape(block, quarter)
            start = pl.multiple_of(which * tokens + i * block, block)
            full[pl.ds(start, block), :] = pair.astype(BF16)
            return carry

        lax.fori_loop(0, chips, step, 0, unroll=True)

    def gather_sent(buffer, send):
        wait_all(buffer.at[pl.ds(0, 2 * count - 1)], send)

    def attention():
        send_version.start()
        send_wo.start()
        send_wv.start()
        loads[0].wait()
        loads[1].wait()
        row = lax.broadcasted_iota(jnp.int32, (tokens, tokens), 0)
        causal = lax.broadcasted_iota(jnp.int32, (tokens, tokens), 1) <= row
        for head in range(heads):
            part = slice(head * HEAD_DIM, (head + 1) * HEAD_DIM)
            scores = dot(query[part], key[part], 0, 0) * (1.0 / math.sqrt(HEAD_DIM))
            scores = jnp.where(causal, scores, -jnp.inf)
            expo = jnp.exp(scores - jnp.max(scores, axis=1, keepdims=True))
            attend = expo / jnp.sum(expo, axis=1, keepdims=True)
            probs[mine, head] = attend.astype(BF16)
        send_probs.start()
        for load in loads[2:]:
            load.wait()
        send_wo.wait_recv()
        send_wv.wait_recv()
        send_version.wait_recv()
        return [jnp.max(versions[which]) for which in range(2)]

    def token_rows(which):
        return slice(which * tokens, (which + 1) * tokens)

    def chain(weight, full, part, cast, sib, total, sent, got, out, side, first_sib, first_pair):
        def first_copy(which):
            return to_sibling(cast.at[which, sib_rows], sib.at[which], first_sib + which)

        def second_copy(which):
            return to_partner(sent.at[which], got.at[which], first_pair + which)

        def third_copy(which):
            place = out.at[own_rows, token_rows(which)]
            return to_sibling(place, place, first_sib + 2 + which)

        def first(which, version):
            product = dot(weight[version], full[token_rows(which)], 1, 1)
            part[which] = product
            cast[which] = product.astype(BF16)
            first_copy(which).start()

        def second(which):
            first_copy(which).wait_recv()
            chip_sum = part[which, own_rows] + sib[which].astype(F32)
            total[which] = chip_sum
            sent[which] = chip_sum.astype(BF16)
            second_copy(which).start()

        def third(which):
            second_copy(which).wait_recv()
            for head in range(heads):
                block_rows = slice(head * HEAD_DIM, (head + 1) * HEAD_DIM)
                whole = total[which, block_rows] + got[which, block_rows].astype(F32)
                mixed = dot(whole.astype(BF16), probs[which, head], 1, side)
                start = pl.multiple_of(core * rows + head * HEAD_DIM, 16)
                out[pl.ds(start, HEAD_DIM), token_rows(which)] = mixed.astype(BF16)
            third_copy(which).start()

        def last(which):
            third_copy(which).wait_recv()

        def sent_wait():
            for which in range(2):
                first_copy(which).wait_send()
                second_copy(which).wait_send()
                third_copy(which).wait_send()

        return first, second, third, last, sent_wait

    x_chain = chain(
        wv, x_full, part_x, cast_x, sib_x, total_x, sent_x, got_x, context, 1, 2, 2
    )
    grad_chain = chain(
        wo, grad_full, part_g, cast_g, sib_g, total_g, sent_g, got_g, value_grad, 0, 6, 4
    )

    def context_phase(chosen, before_third=lambda: None):
        first, second, third, last, _ = x_chain
        for which in range(2):
            gather_wait(x_in, x_full, x_recv, which)
            first(which, chosen[which])
        for which in range(2):
            second(which)
        before_third()
        for which in range(2):
            third(which)
        for which in range(2):
            last(which)

    def gradient_phase(chosen, arrive, deliver, before_third=lambda: None):
        first, second, third, last, _ = grad_chain
        for which in range(2):
            arrive(which)
            first(which, chosen[which])
        for which in range(2):
            second(which)
        before_third()
        for which in range(2):
            third(which)
        for which in range(2):
            last(which)
            deliver(
                which, dot(value_grad[:, token_rows(which)], wv[chosen[which]], 0, 0)
            )

    send_gv = to_sibling(gv_sent, gv_ref.at[0, :, columns(0, core)], 10)
    send_go = to_sibling(go_sent, go_ref.at[0, :, columns(0, core)], 11)
    store_gv = pltpu.make_async_copy(gv, gv_ref.at[0, :, columns(0, core)], out_sem.at[1])
    store_go = pltpu.make_async_copy(go, go_ref.at[0, :, columns(0, core)], out_sem.at[2])
    store_dx = pltpu.make_async_copy(dx_own, dx_ref.at[0], out_sem.at[0])

    def weight_phase():
        for terms, full, kept, sent, store, send in (
            (value_grad, x_full, gv, gv_sent, store_gv, send_gv),
            (context, grad_full, go, go_sent, store_go, send_go),
        ):
            sent[...] = dot(terms[sib_rows], full[...], 1, 0).astype(BF16)
            send.start()
            kept[...] = dot(terms[own_rows], full[...], 1, 0).astype(BF16)
            store.start()

    def chip_rows(which, place):
        return pl.ds(pl.multiple_of(which * tokens + place * block, block), block)

    def shift(which):
        return remote(
            reduced.at[which], shifted.at[which],
            shift_send.at[which], shift_recv.at[which], other, tensor,
        )

    def hand_over():
        return remote(dx_own, grad_own, own_send, own_recv, other, tensor)

    def quarter_columns(place):
        return slice(place * quarter, (place + 1) * quarter)

    def odd_section():
        gather_start(incoming_ref.at[0], grad_in, grad_send, grad_recv)
        chosen = attention()

        def arrive(which):
            gather_wait(grad_in, grad_full, grad_recv, which)

        def deliver(which, product):
            parts_odd[token_rows(which)] = product.astype(BF16)
            slot = got_odd.at[which * chips + chip]
            for dy, dx in offsets:
                place = chip_at(dy, dx)
                source = parts_odd.at[chip_rows(which, place)]
                if dy or dx:
                    remote(
                        source, slot, dx_send, dx_recv.at[which], section, 2 * place + core
                    ).start()
                else:
                    pltpu.make_async_copy(source, slot, dx_recv.at[which]).start()

        gradient_phase(chosen, arrive, deliver, send_probs.wait_recv)
        for which in range(2):
            wait_all(got_odd.at[pl.ds(which * chips, chips)], dx_recv.at[which])
            total = got_odd[which * chips].astype(F32)
            for place in range(1, chips):
                total = total + got_odd[which * chips + place].astype(F32)
            total = total + grad_full[chip_rows(which, chip), :].astype(F32)
            result = total.astype(BF16)
            reduced[which] = result
            shift(which).start()
            pieces[which] = total.reshape(2, shard, quarter).astype(BF16)
        gather_start(x_ref.at[0], x_in, x_send, x_recv)
        slot = assembled.at[2 * mine + core]
        pltpu.make_async_copy(pieces.at[mine, core], slot, piece_recv).start()
        for target, line, lane, lane_core in (
            (section, mine, sibling, 1 - core),
            (partner, 1 - mine, tensor, core),
            (partner, 1 - mine, sibling, 1 - core),
        ):
            remote(pieces.at[line, lane_core], slot, piece_send, piece_recv, target, lane).start()
        wait_all(assembled, piece_recv)
        for place in range(4):
            dx_own[:, quarter_columns(place)] = assembled[place]
        store_dx.start()
        hand_over().start()
        context_phase(chosen)
        weight_phase()
        gather_sent(grad_in, grad_send)
        wait_all(got_odd.at[pl.ds(0, 2 * chips - 2)], dx_send)
        for which in range(2):
            shift(which).wait_send()
        wait_all(assembled.at[pl.ds(0, 3)], piece_send)
        hand_over().wait_send()

    def even_section():
        gather_start(x_ref.at[0], x_in, x_send, x_recv)
        chosen = attention()
        context_phase(chosen, send_probs.wait_recv)
        for which in range(2):
            shift(which).wait_recv()
            slot = grad_full.at[chip_rows(which, chip)]
            for dy, dx in offsets:
                if dy or dx:
                    remote(
                        shifted.at[which], slot, grad_send, grad_recv.at[which],
                        section, 2 * chip_at(dy, dx) + core,
                    ).start()
                else:
                    pltpu.make_async_copy(shifted.at[which], slot, grad_recv.at[which]).start()

        def arrive(which):
            wait_all(grad_full.at[token_rows(which)], grad_recv.at[which])

        def deliver(which, product):
            parts_even[which * count:(which + 1) * count] = product.reshape(
                count, shard, quarter
            ).astype(BF16)
            slot = got_even.at[(2 * mine + core) * chips + chip]
            target = base + which
            for dy, dx in offsets:
                for swap in (1, 0):
                    lane = 2 * chip_at(dy, dx) + (1 - core if swap else core)
                    copy = remote(
                        parts_even.at[which * count + lane], slot, dx_send, dx_recv.at[0], target, lane
                    )
                    if dy or dx or swap:
                        copy.start()
                    else:
                        pl.when(mine != which)(copy.start)

        gradient_phase(chosen, arrive, deliver)
        pltpu.make_async_copy(
            parts_even.at[mine * count + tensor],
            got_even.at[(2 * mine + core) * chips + chip],
            dx_recv.at[0],
        ).start()
        weight_phase()
        hand_over().wait_recv()
        wait_all(got_even, dx_recv.at[0])
        for place in range(4):
            total = got_even[place * chips].astype(F32)
            for slot in range(1, chips):
                total = total + got_even[place * chips + slot].astype(F32)
            part = quarter_columns(place)
            dx_own[:, part] = (grad_own[:, part].astype(F32) + total).astype(BF16)
        store_dx.start()
        wait_all(grad_full.at[pl.ds(0, 2 * (chips - 1) * block)], grad_send)
        wait_all(got_even.at[pl.ds(0, 2 * count - 1)], dx_send)

    pl.when(odd == 1)(odd_section)
    pl.when(odd == 0)(even_section)
    gather_sent(x_in, x_send)
    for copy in (send_version, send_probs, send_wo, send_wv):
        copy.wait_send()
    x_chain[4]()
    grad_chain[4]()
    for copy in (send_gv, send_go):
        copy.wait()
    for copy in (store_dx, store_gv, store_go):
        copy.wait()


def on_device(section_input, query, key_stash, incoming, version, w_value, w_out):
    count = lax.axis_size("tensor")
    shard, width = section_input.shape[1:]
    rows, tokens = query.shape[1:]
    half = width // 2
    quarter = half // 2
    heads = rows // HEAD_DIM
    anywhere = pl.BlockSpec(memory_space=pl.ANY)
    weight = pltpu.VMEM((2, 2 * rows, quarter), BF16)
    blocks = pltpu.VMEM((2 * count, shard, quarter), BF16)
    big_blocks = pltpu.VMEM((count, 2 * shard, quarter), BF16)
    full = pltpu.VMEM((2 * tokens, quarter), BF16)
    pair = pltpu.VMEM((2, rows, tokens), BF16)
    chain = [
        pltpu.VMEM((2, 2 * rows, tokens), F32),
        pltpu.VMEM((2, 2 * rows, tokens), BF16),
        pair,
        pltpu.VMEM((2, rows, tokens), F32),
        pair,
        pair,
        pltpu.VMEM((2 * rows, 2 * tokens), BF16),
    ]
    own = pltpu.VMEM((shard, width), BF16)
    result = pltpu.VMEM((rows, quarter), BF16)
    two = pltpu.VMEM((2, 2 * shard, quarter), BF16)
    dma = pltpu.SemaphoreType.DMA
    return pl.pallas_call(
        functools.partial(kernel, count),
        out_shape=(
            jax.ShapeDtypeStruct((1, shard, width), BF16),
            jax.ShapeDtypeStruct((1, rows, half), BF16),
            jax.ShapeDtypeStruct((1, rows, half), BF16),
        ),
        in_specs=[anywhere] * 4 + [pl.BlockSpec(memory_space=pltpu.SMEM)] + [anywhere] * 2,
        out_specs=(anywhere, anywhere, anywhere),
        scratch_shapes=[
            weight, weight,
            pltpu.VMEM((rows, tokens), BF16),
            pltpu.VMEM((rows, tokens), BF16),
            pltpu.VMEM((2, heads, tokens, tokens), BF16),
            pltpu.VMEM((2, 8, 128), jnp.int32),
            blocks, blocks, full, full,
            *chain, *chain,
            full, big_blocks, blocks, blocks,
            two, two,
            pltpu.VMEM((2, 2, shard, quarter), BF16),
            pltpu.VMEM((4, shard, quarter), BF16),
            own, own, result, result, result, result,
            dma((4,)), dma((6,)), dma((6,)), dma((12,)), dma((12,)),
            dma, dma((2,)), dma, dma((2,)), dma, dma((2,)),
            dma((2,)), dma((2,)), dma, dma, dma, dma, dma((3,)),
        ],
        compiler_params=pltpu.CompilerParams(
            collective_id=0, has_side_effects=True, vmem_limit_bytes=60 * 1024 * 1024
        ),
    )(section_input, query, key_stash, incoming, version, w_value, w_out)


def solution(mesh):
    split = P("section", "tensor", None)
    weights = P("section", None, "tensor", None)
    return jax.shard_map(
        on_device,
        mesh=mesh,
        in_specs=(split, split, split, split, P("section"), weights, weights),
        out_specs=(split, split, split),
        check_vma=False,
    )
```

time: 82.2 us -> 59.7 us (0.73)
  Pallas kernels: 72.5 us -> 54 us
  local copies, waits for them, and re-layouts: 7.98 us -> 4.22 us
    pallas_call x1, Pallas kernels: 72.5 us -> 54 us  [on_device(): pl.pallas_call(functools.partial(kernel, count), out_shape=(jax.ShapeDtyp...]
    unnamed x15 -> x5, local copies, waits for them, and re-layouts: 7.98 us -> 4.22 us
where the time goes in v2:
time: 59.7 us; the launch traced here: 59.6 us
  Pallas kernels  54 us (90%)
  local copies, waits for them, and re-layouts  4.22 us (7%)
  between operations  1.3 us (2%)
    pallas_call x1, Pallas kernels, on_device(): pl.pallas_call(functools.partial(kernel, count), out_shape=(jax.ShapeDtyp...  54 us
    unnamed x5, local copies, waits for them, and re-layouts  4.22 us

profile of v2, /device:TPU:1, one launch (start us, length us, event | category | flops | bytes accessed | tf_op | source)
XLA Modules:
  0.0 59.6 jit_solution(7078654074889329230)
XLA Ops:
  1.3 54.0 %shard_map.94 = (bf16[1,8,3072]{2,1,0:T(8,128)(2,1)}, bf16[1,192,1536]{2,1,0:T(8,128)(2,1)}, bf16[1,192,1536]{2,1,0:T(8,128)(2,1)}) custom-call(bf16[1,8,3072]{2,1,0:T(8,128)(2,1)} %x_ref.1, bf16[1,192,128]{2,1,0:T(8,128)(2,1)} %query_ref.1, bf16[1,192,128]{2,1,0:T(8,128)(2,1)} %key_ref.1, bf16[1,8,3072]{2,1,0:T(8,128)(2,1)} %incoming_ref.1, ...), custom_call_target="tpu_custom_call" | custom-call | tf_op jit(solution)/shard_map/pallas_call | solution.py:445
  55.3 0.0 copy-start
  55.3 1.5 %copy.14 = bf16[1,8,3072]{2,1,0:T(8,128)(2,1)} copy(bf16[1,8,3072]{2,1,0:T(8,128)(2,1)} %get-tuple-element.6) | data formatting | bytes 98304
  56.8 1.9 %copy.15 = bf16[1,192,1536]{2,1,0:T(8,128)(2,1)} copy(bf16[1,192,1536]{2,1,0:T(8,128)(2,1)} %get-tuple-element.7) | data formatting | bytes 1179648
  58.7 0.0 copy-done
  58.7 0.8 %copy.16 = bf16[1,192,1536]{2,1,0:T(8,128)(2,1)} copy(bf16[1,192,1536]{2,1,0:T(8,128)(2,1)S(1)} %copy-done) | data formatting | bytes 1179648
Async XLA Ops:
  55.3 3.4 %copy-start = (bf16[1,192,1536]{2,1,0:T(8,128)(2,1)S(1)}, bf16[1,192,1536]{2,1,0:T(8,128)(2,1)}, u32[]{:S(2)}) copy-start(bf16[1,192,1536]{2,1,0:T(8,128)(2,1)} %get-tuple-element.8) | copy-start | bytes 1769476

commit v3 on v2

--- a/solution.py
+++ b/solution.py
@@ -29,10 +29,10 @@
     part_x, cast_x, sib_x, total_x, sent_x, got_x, context,
     part_g, cast_g, sib_g, total_g, sent_g, got_g, value_grad,
     parts_odd, got_odd, parts_even, got_even,
-    reduced, shifted, pieces, assembled, dx_own, grad_own, gv, go, gv_sent, go_sent,
+    reduced, shifted, pieces, assembled, grad_own, gv_sent, go_sent,
     load_sem, pair_send, pair_recv, sib_send, sib_recv,
     x_send, x_recv, grad_send, grad_recv, dx_send, dx_recv,
-    shift_send, shift_recv, piece_send, piece_recv, own_send, own_recv, out_sem,
+    shift_send, shift_recv, piece_send, piece_recv, own_send, own_recv,
 ):
     section = lax.axis_index("section")
     tensor = lax.axis_index("tensor")
@@ -265,19 +265,15 @@
 
     send_gv = to_sibling(gv_sent, gv_ref.at[0, :, columns(0, core)], 10)
     send_go = to_sibling(go_sent, go_ref.at[0, :, columns(0, core)], 11)
-    store_gv = pltpu.make_async_copy(gv, gv_ref.at[0, :, columns(0, core)], out_sem.at[1])
-    store_go = pltpu.make_async_copy(go, go_ref.at[0, :, columns(0, core)], out_sem.at[2])
-    store_dx = pltpu.make_async_copy(dx_own, dx_ref.at[0], out_sem.at[0])
 
     def weight_phase():
-        for terms, full, kept, sent, store, send in (
-            (value_grad, x_full, gv, gv_sent, store_gv, send_gv),
-            (context, grad_full, go, go_sent, store_go, send_go),
+        for terms, full, kept, sent, send in (
+            (value_grad, x_full, gv_ref, gv_sent, send_gv),
+            (context, grad_full, go_ref, go_sent, send_go),
         ):
             sent[...] = dot(terms[sib_rows], full[...], 1, 0).astype(BF16)
             send.start()
-            kept[...] = dot(terms[own_rows], full[...], 1, 0).astype(BF16)
-            store.start()
+            kept[0, :, columns(0, core)] = dot(terms[own_rows], full[...], 1, 0).astype(BF16)
 
     def chip_rows(which, place):
         return pl.ds(pl.multiple_of(which * tokens + place * block, block), block)
@@ -289,7 +285,7 @@
         )
 
     def hand_over():
-        return remote(dx_own, grad_own, own_send, own_recv, other, tensor)
+        return remote(dx_ref.at[0], grad_own, own_send, own_recv, other, tensor)
 
     def quarter_columns(place):
         return slice(place * quarter, (place + 1) * quarter)
@@ -336,8 +332,7 @@
             remote(pieces.at[line, lane_core], slot, piece_send, piece_recv, target, lane).start()
         wait_all(assembled, piece_recv)
         for place in range(4):
-            dx_own[:, quarter_columns(place)] = assembled[place]
-        store_dx.start()
+            dx_ref[0, :, quarter_columns(place)] = assembled[place]
         hand_over().start()
         context_phase(chosen)
         weight_phase()
@@ -398,8 +393,7 @@
             for slot in range(1, chips):
                 total = total + got_even[place * chips + slot].astype(F32)
             part = quarter_columns(place)
-            dx_own[:, part] = (grad_own[:, part].astype(F32) + total).astype(BF16)
-        store_dx.start()
+            dx_ref[0, :, part] = (grad_own[:, part].astype(F32) + total).astype(BF16)
         wait_all(grad_full.at[pl.ds(0, 2 * (chips - 1) * block)], grad_send)
         wait_all(got_even.at[pl.ds(0, 2 * count - 1)], dx_send)
 
@@ -412,7 +406,16 @@
     grad_chain[4]()
     for copy in (send_gv, send_go):
         copy.wait()
-    for copy in (store_dx, store_gv, store_go):
+
+
+def store_kernel(dx, gv, go, dx_out, gv_out, go_out, sem):
+    copies = [
+        pltpu.make_async_copy(source, result, sem.at[index])
+        for index, (source, result) in enumerate(((dx, dx_out), (gv, gv_out), (go, go_out)))
+    ]
+    for copy in copies:
+        copy.start()
+    for copy in copies:
         copy.wait()
 
 
@@ -423,7 +426,8 @@
     half = width // 2
     quarter = half // 2
     heads = rows // HEAD_DIM
-    anywhere = pl.BlockSpec(memory_space=pl.ANY)
+    hbm = pl.BlockSpec(memory_space=pltpu.HBM)
+    local = pl.BlockSpec(memory_space=pltpu.VMEM)
     weight = pltpu.VMEM((2, 2 * rows, quarter), BF16)
     blocks = pltpu.VMEM((2 * count, shard, quarter), BF16)
     big_blocks = pltpu.VMEM((count, 2 * shard, quarter), BF16)
@@ -442,15 +446,12 @@
     result = pltpu.VMEM((rows, quarter), BF16)
     two = pltpu.VMEM((2, 2 * shard, quarter), BF16)
     dma = pltpu.SemaphoreType.DMA
-    return pl.pallas_call(
+    shapes = ((1, shard, width), (1, rows, half), (1, rows, half))
+    results = pl.pallas_call(
         functools.partial(kernel, count),
-        out_shape=(
-            jax.ShapeDtypeStruct((1, shard, width), BF16),
-            jax.ShapeDtypeStruct((1, rows, half), BF16),
-            jax.ShapeDtypeStruct((1, rows, half), BF16),
-        ),
-        in_specs=[anywhere] * 4 + [pl.BlockSpec(memory_space=pltpu.SMEM)] + [anywhere] * 2,
-        out_specs=(anywhere, anywhere, anywhere),
+        out_shape=tuple(pltpu.VMEM(shape, BF16) for shape in shapes),
+        in_specs=[hbm] * 4 + [pl.BlockSpec(memory_space=pltpu.SMEM)] + [hbm] * 2,
+        out_specs=(local, local, local),
         scratch_shapes=[
             weight, weight,
             pltpu.VMEM((rows, tokens), BF16),
@@ -463,15 +464,23 @@
             two, two,
             pltpu.VMEM((2, 2, shard, quarter), BF16),
             pltpu.VMEM((4, shard, quarter), BF16),
-            own, own, result, result, result, result,
+            own, result, result,
             dma((4,)), dma((6,)), dma((6,)), dma((12,)), dma((12,)),
             dma, dma((2,)), dma, dma((2,)), dma, dma((2,)),
-            dma((2,)), dma((2,)), dma, dma, dma, dma, dma((3,)),
+            dma((2,)), dma((2,)), dma, dma, dma, dma,
         ],
         compiler_params=pltpu.CompilerParams(
-            collective_id=0, has_side_effects=True, vmem_limit_bytes=60 * 1024 * 1024
+            collective_id=0, has_side_effects=True, vmem_limit_bytes=56 * 1024 * 1024
         ),
     )(section_input, query, key_stash, incoming, version, w_value, w_out)
+    return pl.pallas_call(
+        store_kernel,
+        out_shape=tuple(jax.ShapeDtypeStruct(shape, BF16) for shape in shapes),
+        in_specs=[local] * 3,
+        out_specs=(hbm, hbm, hbm),
+        scratch_shapes=[dma((3,))],
+        compiler_params=pltpu.CompilerParams(vmem_limit_bytes=4 * 1024 * 1024),
+    )(*results)
 
 
 def solution(mesh):

time: 59.7 us -> 55.9 us (0.936)
  local copies, waits for them, and re-layouts: 4.22 us -> 0 us
    unnamed x5 -> x0, local copies, waits for them, and re-layouts: 4.22 us -> none
    pallas_call x1 -> x2, Pallas kernels: 54 us -> 54.5 us  [the longest x1 53.4 us: on_device(): pl.pallas_call(functools.partial(kernel, count), out_shape=tuple((pltpu.V...]
where the time goes in v3:
time: 55.9 us; the launch traced here: 55.8 us
  Pallas kernels  54.5 us (97%)
  between operations  1.29 us (2%)
    pallas_call x1, Pallas kernels, on_device(): pl.pallas_call(functools.partial(kernel, count), out_shape=tuple((pltpu.V...  53.4 us

profile of v3, /device:TPU:1, one launch (start us, length us, event | category | flops | bytes accessed | tf_op | source)
XLA Modules:
  0.0 55.8 jit_solution(11746290505281577740)
XLA Ops:
  1.3 53.4 %shard_map.94 = (bf16[1,8,3072]{2,1,0:T(8,128)(2,1)S(1)}, bf16[1,192,1536]{2,1,0:T(8,128)(2,1)S(1)}, bf16[1,192,1536]{2,1,0:T(8,128)(2,1)S(1)}) custom-call(bf16[1,8,3072]{2,1,0:T(8,128)(2,1)} %x_ref.1, bf16[1,192,128]{2,1,0:T(8,128)(2,1)} %query_ref.1, bf16[1,192,128]{2,1,0:T(8,128)(2,1)} %key_ref.1, bf16[1,8,3072]{2,1,0:T(8,128)(2,1)} %incoming_ref.1, ...), custom_call_target="tpu_custom_call" | custom-call | tf_op jit(solution)/shard_map/pallas_call | solution.py:450
  54.7 1.1 %shard_map.95 = (bf16[1,8,3072]{2,1,0:T(8,128)(2,1)}, bf16[1,192,1536]{2,1,0:T(8,128)(2,1)}, bf16[1,192,1536]{2,1,0:T(8,128)(2,1)}) custom-call(bf16[1,8,3072]{2,1,0:T(8,128)(2,1)S(1)} %get-tuple-element.6.dx, bf16[1,192,1536]{2,1,0:T(8,128)(2,1)S(1)} %get-tuple-element.7.gv, bf16[1,192,1536]{2,1,0:T(8,128)(2,1)S(1)} %get-tuple-element.8.go), custom_call_target="tpu_custom_call" | custom-call | tf_op jit(solution)/shard_map/pallas_call | solution.py:476

commit v4 on v3

--- a/solution.py
+++ b/solution.py
@@ -9,6 +9,7 @@
 from jax.sharding import PartitionSpec as P
 
 HEAD_DIM = 96
+CUTS = 2
 BF16 = jnp.bfloat16
 F32 = jnp.float32
 MESH = pl.DeviceIdType.MESH
@@ -29,7 +30,7 @@
     part_x, cast_x, sib_x, total_x, sent_x, got_x, context,
     part_g, cast_g, sib_g, total_g, sent_g, got_g, value_grad,
     parts_odd, got_odd, parts_even, got_even,
-    reduced, shifted, pieces, assembled, grad_own, gv_sent, go_sent,
+    reduced, shifted, pieces, assembled, row, grad_own, gv_sent, go_sent,
     load_sem, pair_send, pair_recv, sib_send, sib_recv,
     x_send, x_recv, grad_send, grad_recv, dx_send, dx_recv,
     shift_send, shift_recv, piece_send, piece_recv, own_send, own_recv,
@@ -97,6 +98,10 @@
             wv_ref.at[0, :, :, columns(0, core)], wv.at[:, own_rows], load_sem.at[3]
         ),
     ]
+    load_incoming = pltpu.make_async_copy(incoming_ref.at[0], row, load_sem.at[4])
+    load_x = pltpu.make_async_copy(x_ref.at[0], row, load_sem.at[4])
+    pl.when(odd == 1)(load_incoming.start)
+    pl.when(odd == 0)(load_x.start)
     for load in loads:
         load.start()
     versions[mine] = jnp.full(versions.shape[1:], version_ref[0], jnp.int32)
@@ -106,16 +111,14 @@
     def signal(target, lane):
         pl.semaphore_signal(barrier, inc=1, device_id=(target, lane), device_id_type=MESH)
 
-    def greet(target, first):
-        def step(j, carry):
-            signal(target, lax.rem(tensor + j, count))
-            return carry
-
-        lax.fori_loop(first, count, step, 0)
-
+    for dy, dx in offsets:
+        place = chip_at(dy, dx)
+        for swap in (1, 0):
+            lane = 2 * place + (1 - core if swap else core)
+            signal(partner, lane)
+            if dy or dx or swap:
+                signal(section, lane)
     signal(other, tensor)
-    greet(partner, 0)
-    greet(section, 1)
     pl.semaphore_wait(barrier, 2 * count)
 
     send_version = to_partner(versions.at[mine], versions.at[mine], 0)
@@ -162,8 +165,8 @@
         send_wv.start()
         loads[0].wait()
         loads[1].wait()
-        row = lax.broadcasted_iota(jnp.int32, (tokens, tokens), 0)
-        causal = lax.broadcasted_iota(jnp.int32, (tokens, tokens), 1) <= row
+        line = lax.broadcasted_iota(jnp.int32, (tokens, tokens), 0)
+        causal = lax.broadcasted_iota(jnp.int32, (tokens, tokens), 1) <= line
         for head in range(heads):
             part = slice(head * HEAD_DIM, (head + 1) * HEAD_DIM)
             scores = dot(query[part], key[part], 0, 0) * (1.0 / math.sqrt(HEAD_DIM))
@@ -249,19 +252,24 @@
 
     def gradient_phase(chosen, arrive, deliver, before_third=lambda: None):
         first, second, third, last, _ = grad_chain
-        for which in range(2):
-            arrive(which)
-            first(which, chosen[which])
-        for which in range(2):
-            second(which)
+        def last_step(which):
+            last(which)
+            weight = wv.at[chosen[which]]
+            deliver(
+                which, lambda part: dot(value_grad[:, token_rows(which)], weight[:, part], 0, 0)
+            )
+
+        arrive(0)
+        first(0, chosen[0])
+        second(0)
+        arrive(1)
+        first(1, chosen[1])
+        second(1)
         before_third()
-        for which in range(2):
-            third(which)
-        for which in range(2):
-            last(which)
-            deliver(
-                which, dot(value_grad[:, token_rows(which)], wv[chosen[which]], 0, 0)
-            )
+        third(0)
+        last_step(0)
+        third(1)
+        last_step(1)
 
     send_gv = to_sibling(gv_sent, gv_ref.at[0, :, columns(0, core)], 10)
     send_go = to_sibling(go_sent, go_ref.at[0, :, columns(0, core)], 11)
@@ -278,10 +286,16 @@
     def chip_rows(which, place):
         return pl.ds(pl.multiple_of(which * tokens + place * block, block), block)
 
-    def shift(which):
+    def cut_columns(cut):
+        return slice(cut * (quarter // CUTS), (cut + 1) * (quarter // CUTS))
+
+    all_cuts = [(which, cut) for which in range(2) for cut in range(CUTS)]
+
+    def shift(which, cut):
+        place = which * CUTS + cut
         return remote(
-            reduced.at[which], shifted.at[which],
-            shift_send.at[which], shift_recv.at[which], other, tensor,
+            reduced.at[which, :, cut_columns(cut)], shifted.at[which, :, cut_columns(cut)],
+            shift_send.at[place], shift_recv.at[place], other, tensor,
         )
 
     def hand_over():
@@ -291,36 +305,39 @@
         return slice(place * quarter, (place + 1) * quarter)
 
     def odd_section():
-        gather_start(incoming_ref.at[0], grad_in, grad_send, grad_recv)
+        load_incoming.wait()
+        gather_start(row, grad_in, grad_send, grad_recv)
         chosen = attention()
 
         def arrive(which):
             gather_wait(grad_in, grad_full, grad_recv, which)
 
-        def deliver(which, product):
-            parts_odd[token_rows(which)] = product.astype(BF16)
-            slot = got_odd.at[which * chips + chip]
-            for dy, dx in offsets:
-                place = chip_at(dy, dx)
-                source = parts_odd.at[chip_rows(which, place)]
-                if dy or dx:
-                    remote(
-                        source, slot, dx_send, dx_recv.at[which], section, 2 * place + core
-                    ).start()
-                else:
-                    pltpu.make_async_copy(source, slot, dx_recv.at[which]).start()
+        def deliver(which, multiply):
+            for cut in range(CUTS):
+                parts_odd[token_rows(which), cut_columns(cut)] = multiply(cut_columns(cut)).astype(BF16)
+                slot = got_odd.at[which * chips + chip, :, cut_columns(cut)]
+                arrived = dx_recv.at[which * CUTS + cut]
+                for dy, dx in offsets:
+                    place = chip_at(dy, dx)
+                    source = parts_odd.at[chip_rows(which, place), cut_columns(cut)]
+                    if dy or dx:
+                        remote(source, slot, dx_send, arrived, section, 2 * place + core).start()
+                    else:
+                        pltpu.make_async_copy(source, slot, arrived).start()
 
         gradient_phase(chosen, arrive, deliver, send_probs.wait_recv)
-        for which in range(2):
-            wait_all(got_odd.at[pl.ds(which * chips, chips)], dx_recv.at[which])
-            total = got_odd[which * chips].astype(F32)
+        for which, cut in all_cuts:
+            part = cut_columns(cut)
+            wait_all(
+                got_odd.at[pl.ds(which * chips, chips), :, part], dx_recv.at[which * CUTS + cut]
+            )
+            total = got_odd[which * chips, :, part].astype(F32)
             for place in range(1, chips):
-                total = total + got_odd[which * chips + place].astype(F32)
-            total = total + grad_full[chip_rows(which, chip), :].astype(F32)
-            result = total.astype(BF16)
-            reduced[which] = result
-            shift(which).start()
-            pieces[which] = total.reshape(2, shard, quarter).astype(BF16)
+                total = total + got_odd[which * chips + place, :, part].astype(F32)
+            total = total + grad_full[chip_rows(which, chip), part].astype(F32)
+            reduced[which, :, part] = total.astype(BF16)
+            shift(which, cut).start()
+            pieces[which, :, :, part] = total.reshape(2, shard, quarter // CUTS).astype(BF16)
         gather_start(x_ref.at[0], x_in, x_send, x_recv)
         slot = assembled.at[2 * mine + core]
         pltpu.make_async_copy(pieces.at[mine, core], slot, piece_recv).start()
@@ -338,31 +355,34 @@
         weight_phase()
         gather_sent(grad_in, grad_send)
         wait_all(got_odd.at[pl.ds(0, 2 * chips - 2)], dx_send)
-        for which in range(2):
-            shift(which).wait_send()
+        for which, cut in all_cuts:
+            shift(which, cut).wait_send()
         wait_all(assembled.at[pl.ds(0, 3)], piece_send)
         hand_over().wait_send()
 
     def even_section():
-        gather_start(x_ref.at[0], x_in, x_send, x_recv)
+        load_x.wait()
+        gather_start(row, x_in, x_send, x_recv)
         chosen = attention()
         context_phase(chosen, send_probs.wait_recv)
-        for which in range(2):
-            shift(which).wait_recv()
-            slot = grad_full.at[chip_rows(which, chip)]
+        for which, cut in all_cuts:
+            shift(which, cut).wait_recv()
+            source = shifted.at[which, :, cut_columns(cut)]
+            slot = grad_full.at[chip_rows(which, chip), cut_columns(cut)]
             for dy, dx in offsets:
                 if dy or dx:
                     remote(
-                        shifted.at[which], slot, grad_send, grad_recv.at[which],
+                        source, slot, grad_send, grad_recv.at[which],
                         section, 2 * chip_at(dy, dx) + core,
                     ).start()
                 else:
-                    pltpu.make_async_copy(shifted.at[which], slot, grad_recv.at[which]).start()
+                    pltpu.make_async_copy(source, slot, grad_recv.at[which]).start()
 
         def arrive(which):
             wait_all(grad_full.at[token_rows(which)], grad_recv.at[which])
 
-        def deliver(which, product):
+        def deliver(which, multiply):
+            product = multiply(slice(None))
             parts_even[which * count:(which + 1) * count] = product.reshape(
                 count, shard, quarter
             ).astype(BF16)
@@ -464,10 +484,10 @@
             two, two,
             pltpu.VMEM((2, 2, shard, quarter), BF16),
             pltpu.VMEM((4, shard, quarter), BF16),
-            own, result, result,
-            dma((4,)), dma((6,)), dma((6,)), dma((12,)), dma((12,)),
-            dma, dma((2,)), dma, dma((2,)), dma, dma((2,)),
-            dma((2,)), dma((2,)), dma, dma, dma, dma,
+            own, own, result, result,
+            dma((5,)), dma((6,)), dma((6,)), dma((12,)), dma((12,)),
+            dma, dma((2,)), dma, dma((2,)), dma, dma((2 * CUTS,)),
+            dma((2 * CUTS,)), dma((2 * CUTS,)), dma, dma, dma, dma,
         ],
         compiler_params=pltpu.CompilerParams(
             collective_id=0, has_side_effects=True, vmem_limit_bytes=56 * 1024 * 1024

time: 55.9 us -> 53.5 us (0.957)
  Pallas kernels: 54.5 us -> 52.1 us
    pallas_call x1, Pallas kernels: 53.4 us -> 51.1 us  [on_device(): pl.pallas_call(functools.partial(kernel, count), out_shape=tuple((pltpu.V...]
where the time goes in v4:
time: 53.5 us; the launch traced here: 53.4 us
  Pallas kernels  52.1 us (97%)
  between operations  1.29 us (2%)
    pallas_call x1, Pallas kernels, on_device(): pl.pallas_call(functools.partial(kernel, count), out_shape=tuple((pltpu.V...  51.1 us

profile of v4, /device:TPU:1, one launch (start us, length us, event | category | flops | bytes accessed | tf_op | source)
XLA Modules:
  0.0 53.4 jit_solution(1057180863614013899)
XLA Ops:
  1.3 51.1 %shard_map.94 = (bf16[1,8,3072]{2,1,0:T(8,128)(2,1)S(1)}, bf16[1,192,1536]{2,1,0:T(8,128)(2,1)S(1)}, bf16[1,192,1536]{2,1,0:T(8,128)(2,1)S(1)}) custom-call(bf16[1,8,3072]{2,1,0:T(8,128)(2,1)} %x_ref.1, bf16[1,192,128]{2,1,0:T(8,128)(2,1)} %query_ref.1, bf16[1,192,128]{2,1,0:T(8,128)(2,1)} %key_ref.1, bf16[1,8,3072]{2,1,0:T(8,128)(2,1)} %incoming_ref.1, ...), custom_call_target="tpu_custom_call" | custom-call | tf_op jit(solution)/shard_map/pallas_call | solution.py:470
  52.4 1.1 %shard_map.95 = (bf16[1,8,3072]{2,1,0:T(8,128)(2,1)}, bf16[1,192,1536]{2,1,0:T(8,128)(2,1)}, bf16[1,192,1536]{2,1,0:T(8,128)(2,1)}) custom-call(bf16[1,8,3072]{2,1,0:T(8,128)(2,1)S(1)} %get-tuple-element.6.dx, bf16[1,192,1536]{2,1,0:T(8,128)(2,1)S(1)} %get-tuple-element.7.gv, bf16[1,192,1536]{2,1,0:T(8,128)(2,1)S(1)} %get-tuple-element.8.go), custom_call_target="tpu_custom_call" | custom-call | tf_op jit(solution)/shard_map/pallas_call | solution.py:496

commit v5 on v4

--- a/solution.py
+++ b/solution.py
@@ -31,7 +31,7 @@
     part_g, cast_g, sib_g, total_g, sent_g, got_g, value_grad,
     parts_odd, got_odd, parts_even, got_even,
     reduced, shifted, pieces, assembled, row, grad_own, gv_sent, go_sent,
-    load_sem, pair_send, pair_recv, sib_send, sib_recv,
+    ready_sem, load_sem, pair_send, pair_recv, sib_send, sib_recv,
     x_send, x_recv, grad_send, grad_recv, dx_send, dx_recv,
     shift_send, shift_recv, piece_send, piece_recv, own_send, own_recv,
 ):
@@ -102,10 +102,6 @@
     load_x = pltpu.make_async_copy(x_ref.at[0], row, load_sem.at[4])
     pl.when(odd == 1)(load_incoming.start)
     pl.when(odd == 0)(load_x.start)
-    for load in loads:
-        load.start()
-    versions[mine] = jnp.full(versions.shape[1:], version_ref[0], jnp.int32)
-
     barrier = pltpu.get_barrier_semaphore()
 
     def signal(target, lane):
@@ -118,8 +114,16 @@
             signal(partner, lane)
             if dy or dx or swap:
                 signal(section, lane)
-    signal(other, tensor)
-    pl.semaphore_wait(barrier, 2 * count)
+    pl.when(odd == 1)(lambda: signal(other, tensor))
+    for load in loads:
+        load.start()
+    versions[mine] = jnp.full(versions.shape[1:], version_ref[0], jnp.int32)
+    pl.semaphore_wait(barrier, 2 * count - odd)
+    pl.when(odd == 0)(
+        lambda: pl.semaphore_signal(
+            ready_sem, inc=1, device_id=(other, tensor), device_id_type=MESH
+        )
+    )
 
     send_version = to_partner(versions.at[mine], versions.at[mine], 0)
     send_probs = to_partner(probs.at[mine], probs.at[mine], 1)
@@ -174,7 +178,7 @@
             expo = jnp.exp(scores - jnp.max(scores, axis=1, keepdims=True))
             attend = expo / jnp.sum(expo, axis=1, keepdims=True)
             probs[mine, head] = attend.astype(BF16)
-        send_probs.start()
+        pl.when(odd == 0)(send_probs.start)
         for load in loads[2:]:
             load.wait()
         send_wo.wait_recv()
@@ -196,8 +200,11 @@
             place = out.at[own_rows, token_rows(which)]
             return to_sibling(place, place, first_sib + 2 + which)
 
-        def first(which, version):
-            product = dot(weight[version], full[token_rows(which)], 1, 1)
+        def first(which, version, pieces=None):
+            if pieces is None:
+                product = dot(weight[version], full[token_rows(which)], 1, 1)
+            else:
+                product = pieces(weight.at[version])
             part[which] = product
             cast[which] = product.astype(BF16)
             first_copy(which).start()
@@ -259,12 +266,9 @@
                 which, lambda part: dot(value_grad[:, token_rows(which)], weight[:, part], 0, 0)
             )
 
-        arrive(0)
-        first(0, chosen[0])
-        second(0)
-        arrive(1)
-        first(1, chosen[1])
-        second(1)
+        for which in range(2):
+            first(which, chosen[which], arrive(which))
+            second(which)
         before_third()
         third(0)
         last_step(0)
@@ -304,6 +308,15 @@
     def quarter_columns(place):
         return slice(place * quarter, (place + 1) * quarter)
 
+    def settle():
+        gather_sent(x_in, x_send)
+        for copy in (send_version, send_probs, send_wo, send_wv):
+            copy.wait_send()
+        x_chain[4]()
+        grad_chain[4]()
+        for copy in (send_gv, send_go):
+            copy.wait()
+
     def odd_section():
         load_incoming.wait()
         gather_start(row, grad_in, grad_send, grad_recv)
@@ -311,6 +324,8 @@
 
         def arrive(which):
             gather_wait(grad_in, grad_full, grad_recv, which)
+            if which == 0:
+                send_probs.start()
 
         def deliver(which, multiply):
             for cut in range(CUTS):
@@ -326,6 +341,7 @@
                         pltpu.make_async_copy(source, slot, arrived).start()
 
         gradient_phase(chosen, arrive, deliver, send_probs.wait_recv)
+        pl.semaphore_wait(ready_sem, 1)
         for which, cut in all_cuts:
             part = cut_columns(cut)
             wait_all(
@@ -359,6 +375,7 @@
             shift(which, cut).wait_send()
         wait_all(assembled.at[pl.ds(0, 3)], piece_send)
         hand_over().wait_send()
+        settle()
 
     def even_section():
         load_x.wait()
@@ -372,14 +389,23 @@
             for dy, dx in offsets:
                 if dy or dx:
                     remote(
-                        source, slot, grad_send, grad_recv.at[which],
+                        source, slot, grad_send, grad_recv.at[which * CUTS + cut],
                         section, 2 * chip_at(dy, dx) + core,
                     ).start()
                 else:
-                    pltpu.make_async_copy(source, slot, grad_recv.at[which]).start()
+                    pltpu.make_async_copy(source, slot, grad_recv.at[which * CUTS + cut]).start()
 
         def arrive(which):
-            wait_all(grad_full.at[token_rows(which)], grad_recv.at[which])
+            def pieces(weight):
+                product = None
+                for cut in range(CUTS):
+                    part = cut_columns(cut)
+                    wait_all(grad_full.at[token_rows(which), part], grad_recv.at[which * CUTS + cut])
+                    terms = dot(weight[:, part], grad_full[token_rows(which), part], 1, 1)
+                    product = terms if product is None else product + terms
+                return product
+
+            return pieces
 
         def deliver(which, multiply):
             product = multiply(slice(None))
@@ -392,7 +418,7 @@
                 for swap in (1, 0):
                     lane = 2 * chip_at(dy, dx) + (1 - core if swap else core)
                     copy = remote(
-                        parts_even.at[which * count + lane], slot, dx_send, dx_recv.at[0], target, lane
+                        parts_even.at[which * count + lane], slot, dx_send, dx_recv.at[mine], target, lane
                     )
                     if dy or dx or swap:
                         copy.start()
@@ -403,29 +429,25 @@
         pltpu.make_async_copy(
             parts_even.at[mine * count + tensor],
             got_even.at[(2 * mine + core) * chips + chip],
-            dx_recv.at[0],
+            dx_recv.at[mine],
         ).start()
         weight_phase()
+        settle()
+        wait_all(grad_full.at[pl.ds(0, 2 * (chips - 1) * block)], grad_send)
         hand_over().wait_recv()
-        wait_all(got_even, dx_recv.at[0])
-        for place in range(4):
-            total = got_even[place * chips].astype(F32)
-            for slot in range(1, chips):
-                total = total + got_even[place * chips + slot].astype(F32)
-            part = quarter_columns(place)
-            dx_ref[0, :, part] = (grad_own[:, part].astype(F32) + total).astype(BF16)
-        wait_all(grad_full.at[pl.ds(0, 2 * (chips - 1) * block)], grad_send)
         wait_all(got_even.at[pl.ds(0, 2 * count - 1)], dx_send)
+        for side in (mine, 1 - mine):
+            wait_all(got_even.at[pl.ds(side * count, count)], dx_recv.at[side])
+            for lane_core in range(2):
+                first = side * count + lane_core * chips
+                total = got_even[first].astype(F32)
+                for slot in range(1, chips):
+                    total = total + got_even[first + slot].astype(F32)
+                part = columns(side, lane_core)
+                dx_ref[0, :, part] = (grad_own[:, part].astype(F32) + total).astype(BF16)
 
     pl.when(odd == 1)(odd_section)
     pl.when(odd == 0)(even_section)
-    gather_sent(x_in, x_send)
-    for copy in (send_version, send_probs, send_wo, send_wv):
-        copy.wait_send()
-    x_chain[4]()
-    grad_chain[4]()
-    for copy in (send_gv, send_go):
-        copy.wait()
 
 
 def store_kernel(dx, gv, go, dx_out, gv_out, go_out, sem):
@@ -485,8 +507,9 @@
             pltpu.VMEM((2, 2, shard, quarter), BF16),
             pltpu.VMEM((4, shard, quarter), BF16),
             own, own, result, result,
+            pltpu.SemaphoreType.REGULAR,
             dma((5,)), dma((6,)), dma((6,)), dma((12,)), dma((12,)),
-            dma, dma((2,)), dma, dma((2,)), dma, dma((2 * CUTS,)),
+            dma, dma((2,)), dma, dma((2 * CUTS,)), dma, dma((2 * CUTS,)),
             dma((2 * CUTS,)), dma((2 * CUTS,)), dma, dma, dma, dma,
         ],
         compiler_params=pltpu.CompilerParams(

time: 53.5 us -> 53.2 us (level)
  no operation moved by 1% of the time
where the time goes in v5:
time: 53.2 us; the launch traced here: 52.9 us
  Pallas kernels  51.6 us (97%)
  between operations  1.29 us (2%)
    pallas_call x1, Pallas kernels, on_device(): pl.pallas_call(functools.partial(kernel, count), out_shape=tuple((pltpu.V...  50.5 us

profile of v5, /device:TPU:1, one launch (start us, length us, event | category | flops | bytes accessed | tf_op | source)
XLA Modules:
  0.0 52.9 jit_solution(5672143864097385973)
XLA Ops:
  1.3 50.5 %shard_map.94 = (bf16[1,8,3072]{2,1,0:T(8,128)(2,1)S(1)}, bf16[1,192,1536]{2,1,0:T(8,128)(2,1)S(1)}, bf16[1,192,1536]{2,1,0:T(8,128)(2,1)S(1)}) custom-call(bf16[1,8,3072]{2,1,0:T(8,128)(2,1)} %x_ref.1, bf16[1,192,128]{2,1,0:T(8,128)(2,1)} %query_ref.1, bf16[1,192,128]{2,1,0:T(8,128)(2,1)} %key_ref.1, bf16[1,8,3072]{2,1,0:T(8,128)(2,1)} %incoming_ref.1, ...), custom_call_target="tpu_custom_call" | custom-call | tf_op jit(solution)/shard_map/pallas_call | solution.py:492
  51.8 1.1 %shard_map.95 = (bf16[1,8,3072]{2,1,0:T(8,128)(2,1)}, bf16[1,192,1536]{2,1,0:T(8,128)(2,1)}, bf16[1,192,1536]{2,1,0:T(8,128)(2,1)}) custom-call(bf16[1,8,3072]{2,1,0:T(8,128)(2,1)S(1)} %get-tuple-element.6.dx, bf16[1,192,1536]{2,1,0:T(8,128)(2,1)S(1)} %get-tuple-element.7.gv, bf16[1,192,1536]{2,1,0:T(8,128)(2,1)S(1)} %get-tuple-element.8.go), custom_call_target="tpu_custom_call" | custom-call | tf_op jit(solution)/shard_map/pallas_call | solution.py:519

commit v6 on v5

--- a/solution.py
+++ b/solution.py
@@ -262,8 +262,9 @@
         def last_step(which):
             last(which)
             weight = wv.at[chosen[which]]
+            turned = value_grad[:, token_rows(which)].T
             deliver(
-                which, lambda part: dot(value_grad[:, token_rows(which)], weight[:, part], 0, 0)
+                which, lambda part: dot(turned, weight[:, part], 1, 0)
             )
 
         for which in range(2):

time: 53.2 us -> 53.2 us (level)
  no operation moved by 1% of the time
where the time goes in v6:
time: 53.2 us; the launch traced here: 52.9 us
  Pallas kernels  51.6 us (97%)
  between operations  1.29 us (2%)
    pallas_call x1, Pallas kernels, on_device(): pl.pallas_call(functools.partial(kernel, count), out_shape=tuple((pltpu.V...  50.5 us

profile of v6, /device:TPU:1, one launch (start us, length us, event | category | flops | bytes accessed | tf_op | source)
XLA Modules:
  0.0 52.9 jit_solution(7732466799812861197)
XLA Ops:
  1.3 50.5 %shard_map.94 = (bf16[1,8,3072]{2,1,0:T(8,128)(2,1)S(1)}, bf16[1,192,1536]{2,1,0:T(8,128)(2,1)S(1)}, bf16[1,192,1536]{2,1,0:T(8,128)(2,1)S(1)}) custom-call(bf16[1,8,3072]{2,1,0:T(8,128)(2,1)} %x_ref.1, bf16[1,192,128]{2,1,0:T(8,128)(2,1)} %query_ref.1, bf16[1,192,128]{2,1,0:T(8,128)(2,1)} %key_ref.1, bf16[1,8,3072]{2,1,0:T(8,128)(2,1)} %incoming_ref.1, ...), custom_call_target="tpu_custom_call" | custom-call | tf_op jit(solution)/shard_map/pallas_call | solution.py:493
  51.8 1.1 %shard_map.95 = (bf16[1,8,3072]{2,1,0:T(8,128)(2,1)}, bf16[1,192,1536]{2,1,0:T(8,128)(2,1)}, bf16[1,192,1536]{2,1,0:T(8,128)(2,1)}) custom-call(bf16[1,8,3072]{2,1,0:T(8,128)(2,1)S(1)} %get-tuple-element.6.dx, bf16[1,192,1536]{2,1,0:T(8,128)(2,1)S(1)} %get-tuple-element.7.gv, bf16[1,192,1536]{2,1,0:T(8,128)(2,1)S(1)} %get-tuple-element.8.go), custom_call_target="tpu_custom_call" | custom-call | tf_op jit(solution)/shard_map/pallas_call | solution.py:520

commit v7 on v6

--- a/solution.py
+++ b/solution.py
@@ -437,14 +437,14 @@
         wait_all(grad_full.at[pl.ds(0, 2 * (chips - 1) * block)], grad_send)
         hand_over().wait_recv()
         wait_all(got_even.at[pl.ds(0, 2 * count - 1)], dx_send)
-        for side in (mine, 1 - mine):
+        for side in (0, 1):
             wait_all(got_even.at[pl.ds(side * count, count)], dx_recv.at[side])
             for lane_core in range(2):
                 first = side * count + lane_core * chips
                 total = got_even[first].astype(F32)
                 for slot in range(1, chips):
                     total = total + got_even[first + slot].astype(F32)
-                part = columns(side, lane_core)
+                part = quarter_columns(2 * side + lane_core)
                 dx_ref[0, :, part] = (grad_own[:, part].astype(F32) + total).astype(BF16)
 
     pl.when(odd == 1)(odd_section)

time: 53.2 us -> 53.2 us (level)
  no operation moved by 1% of the time
where the time goes in v7:
time: 53.2 us; the launch traced here: 52.9 us
  Pallas kernels  51.6 us (97%)
  between operations  1.29 us (2%)
    pallas_call x1, Pallas kernels, on_device(): pl.pallas_call(functools.partial(kernel, count), out_shape=tuple((pltpu.V...  50.5 us

profile of v7, /device:TPU:1, one launch (start us, length us, event | category | flops | bytes accessed | tf_op | source)
XLA Modules:
  0.0 52.9 jit_solution(2910677345934546753)
XLA Ops:
  1.3 50.5 %shard_map.94 = (bf16[1,8,3072]{2,1,0:T(8,128)(2,1)S(1)}, bf16[1,192,1536]{2,1,0:T(8,128)(2,1)S(1)}, bf16[1,192,1536]{2,1,0:T(8,128)(2,1)S(1)}) custom-call(bf16[1,8,3072]{2,1,0:T(8,128)(2,1)} %x_ref.1, bf16[1,192,128]{2,1,0:T(8,128)(2,1)} %query_ref.1, bf16[1,192,128]{2,1,0:T(8,128)(2,1)} %key_ref.1, bf16[1,8,3072]{2,1,0:T(8,128)(2,1)} %incoming_ref.1, ...), custom_call_target="tpu_custom_call" | custom-call | tf_op jit(solution)/shard_map/pallas_call | solution.py:493
  51.8 1.1 %shard_map.95 = (bf16[1,8,3072]{2,1,0:T(8,128)(2,1)}, bf16[1,192,1536]{2,1,0:T(8,128)(2,1)}, bf16[1,192,1536]{2,1,0:T(8,128)(2,1)}) custom-call(bf16[1,8,3072]{2,1,0:T(8,128)(2,1)S(1)} %get-tuple-element.6.dx, bf16[1,192,1536]{2,1,0:T(8,128)(2,1)S(1)} %get-tuple-element.7.gv, bf16[1,192,1536]{2,1,0:T(8,128)(2,1)S(1)} %get-tuple-element.8.go), custom_call_target="tpu_custom_call" | custom-call | tf_op jit(solution)/shard_map/pallas_call | solution.py:520
